TPU v7x, 32 devices: a whole 2x2x4 slice. The times are simulated.
32 devices in a mesh: wide: 8 (over y, x, core), narrow: 4 (over z).
Axes of the slice: x: 2, y: 2, z: 4, core: 2. Of those that a mesh axis runs over, the one named last changes fastest.
Arguments:
- coarse_basis: bfloat16 [16, 96, 3, 16, 8, 128], P('wide', None, None, 'narrow')
- material_ids: int32 [16, 16, 8, 128], P('wide', 'narrow'), may hold values from 0 to 15
- lame_table: bfloat16 [2, 16], replicated, may hold values from 0.5 to 4
- coarse_ids: int32 [16, 96], P('wide'), may hold values from 0 to 127, as said below
- coarse_slab: bfloat16 [98304, 512], P('wide', 'narrow'), may hold values from -0.5 to 2.5, as said below
- panel_owner: int32 [1], replicated, may hold values from 0 to 2
Outputs:
- factored: bfloat16 [98304, 512], P('wide', 'narrow')
- galerkin: float32 [16, 96, 96], P('wide')
Inputs may be any that keep to these rules, and one draw needn't show every extreme that they name: `coarse_ids`: the 96 numbers of a row are distinct. `coarse_slab`: for every column block t, the 128 x 128 block whose rows begin at t * 2 * 12288 is symmetric positive definite.
All inputs are finite; a program needn't handle non-finite values.
Results may differ from a plain program's by a relative error of at most 0.001.
The roundings to bfloat16 on the way count: a program that leaves them out, or rounds other values in their place, can miss the bound.
Values may be sent and summed in bfloat16 or wider, within the bound.
No kernel may reach another device: no remote copies, remote signals or barrier semaphores. Data moves between devices by JAX's collectives and lax.ppermute only.
A program may use at most 192 MiB of HBM per device.

v0:
```python
import functools

import jax
import jax.numpy as jnp
from jax import lax
from jax.experimental import pallas as pl
from jax.experimental.pallas import tpu as pltpu
from jax.sharding import PartitionSpec as P

F32, BF16 = jnp.float32, jnp.bfloat16
NT = (((1,), (1,)), ((), ()))
TN = (((0,), (0,)), ((), ()))
VMEM = pl.BlockSpec(memory_space=pltpu.VMEM)
ANY = pl.BlockSpec(memory_space=pl.ANY)
SMEM = pl.BlockSpec(memory_space=pltpu.SMEM)
PLANS = {
    1: (
        (12, 8, 4),
        False,
        True,
        (
            "assemble", "next", "spread", "others", "spread", "more", "spread", (0, 0), "factor", "summary",
            "added", ("panel", 0, 2), "sums", ("panel", 2, 3),
        ),
    ),
    2: (
        (12, 6, 4, 2),
        False,
        True,
        (
            "assemble", "next", "spread", "others", "spread", "more", "spread", (0, 0), (1, 0), "factor", (2, 0),
            "summary", "added", ("panel", 1, 2), (3, 0), ("panel", 0, 1), "sums", ("panel", 2, 4),
        ),
    ),
    3: (
        (12, 8, 4),
        False,
        False,
        (
            "assemble", "next", "spread", "others", "spread", "more", "spread", (0, 0), (1, 0), "factor", (0, 1),
            (2, 0), (1, 1), "summary", "added", (2, 1), ("panel", 1, 2), ("panel", 0, 1), "sums", ("panel", 2, 3),
        ),
    ),
}
BLOCK = 16
LIGHT = pl.CostEstimate(flops=1, bytes_accessed=1, transcendentals=0)


def exact_dot(left, right, dims=(((1,), (0,)), ((), ()))):
    return lax.dot_general(
        left, right, dims, precision=lax.Precision.HIGHEST, preferred_element_type=F32
    )


def dot(left, right, dims=(((1,), (0,)), ((), ()))):
    return lax.dot_general(left, right, dims, preferred_element_type=F32)


def split_two(value):
    high = value.astype(BF16)
    return high, (value - high.astype(F32)).astype(BF16)


def lame_of(ids, table_ref):
    shear = jnp.zeros(ids.shape, F32)
    dilate = jnp.zeros(ids.shape, F32)
    for material in range(table_ref.shape[1]):
        chosen = ids == material
        shear = jnp.where(chosen, table_ref[0, material], shear)
        dilate = jnp.where(chosen, table_ref[1, material], dilate)
    return shear, dilate


def halo_kernel(table_ref, ids_ref, token_ref, basis_ref, slab_ref, out_ref, last_ref, *rest, spans):
    piece_refs, sems = rest[:-1], rest[-1]
    subs, funcs, comps, layers = basis_ref.shape[0:4]
    copies = []
    for number, ((low, high), piece_ref) in enumerate(zip(spans, piece_refs)):
        copies.append(pltpu.make_async_copy(slab_ref.at[pl.ds(low, high - low)], piece_ref, sems.at[number]))
        copies[-1].start()
    for sub in range(subs):
        for comp in range(comps):
            out_ref[sub, comp * funcs : (comp + 1) * funcs] = basis_ref[sub, :, comp, 0]
            last_ref[sub, comp * funcs : (comp + 1) * funcs] = basis_ref[sub, :, comp, layers - 1]
        shear, dilate = lame_of(ids_ref[sub, 0], table_ref)
        out_ref[sub, comps * funcs] = shear.astype(BF16)
        out_ref[sub, comps * funcs + 1] = dilate.astype(BF16)
    for copy in copies:
        copy.wait()


def halo_message(table, ids, token, basis, slab, spans):
    subs, funcs, comps, layers, ny, nz = basis.shape
    return pl.pallas_call(
        functools.partial(halo_kernel, spans=spans),
        in_specs=[SMEM, VMEM, ANY, VMEM, ANY],
        out_specs=[VMEM] * (2 + len(spans)),
        out_shape=[
            jax.ShapeDtypeStruct((subs, comps * funcs + 2, ny, nz), BF16),
            jax.ShapeDtypeStruct((subs, comps * funcs, ny, nz), BF16),
        ]
        + [jax.ShapeDtypeStruct((high - low, slab.shape[1]), BF16) for low, high in spans],
        scratch_shapes=[pltpu.SemaphoreType.DMA((max(1, len(spans)),))],
        compiler_params=pltpu.CompilerParams(vmem_limit_bytes=16 * 2**20),
        cost_estimate=LIGHT,
        name="halo_message",
    )(table, ids, token, basis, slab)


def interior_kernel(edge_ref, table_ref, ids_ref, basis_ref, token_ref, out_ref, fields, turned, coef, left, right, acc):
    sub, comp = pl.program_id(0), pl.program_id(1)
    layers, ny, nz = basis_ref.shape[3:]
    funcs = basis_ref.shape[1]
    row = lax.broadcasted_iota(jnp.int32, (ny, nz), 0)
    lane = lax.broadcasted_iota(jnp.int32, (ny, nz), 1)
    table = [lame_of(ids_ref[sub, x], table_ref) for x in range(layers)]

    def weight(one, two, direction):
        shear = 0.5 * (one[0] + two[0])
        dilate = 0.5 * (one[1] + two[1])
        return shear + jnp.where(comp == direction, shear + dilate, 0.0)

    def ahead(field, axis):
        size = field.shape[axis]
        index = row if axis == 0 else lane
        return jnp.where(index == size - 1, 0.0, pltpu.roll(field, size - 1, axis=axis))

    def behind(field, axis):
        index = row if axis == 0 else lane
        return jnp.where(index == 0, 0.0, pltpu.roll(field, 1, axis=axis))

    nothing = (jnp.zeros((ny, nz), F32),) * 2
    previous = weight(table[0], nothing, 0) * edge_ref[0].astype(F32)
    for x in range(layers):
        diagonal = previous
        forward = []
        if x + 1 < layers:
            face = weight(table[x], table[x + 1], 0)
            diagonal = diagonal + face
            previous = face
            forward.append(face)
        else:
            forward.append(jnp.zeros((ny, nz), F32))
        for axis in (0, 1):
            index, size = (row, ny) if axis == 0 else (lane, nz)
            other = tuple(ahead(value, axis) for value in table[x])
            face = weight(table[x], other, axis + 1)
            before = tuple(behind(value, axis) for value in table[x])
            diagonal = diagonal + face + weight(table[x], before, axis + 1)
            forward.append(jnp.where(index == size - 1, 0.0, face))
        coef[x, 0] = 0.5 * diagonal
        for kind in range(3):
            coef[x, kind + 1] = forward[kind]
        fields[x] = basis_ref[sub, :, comp, x].astype(F32).reshape(funcs * ny, nz)

    total = None
    for x in reversed(range(layers)):
        values = [fields[x, pl.ds(y, funcs, stride=ny), :] for y in range(ny)]
        for y in range(ny):
            value = values[y]
            turned[x % 2, y] = value
            image = coef[x, 0, y : y + 1, :] * value
            image = image - coef[x, 3, y : y + 1, :] * pltpu.roll(value, nz - 1, axis=1)
            if y + 1 < ny:
                image = image - coef[x, 2, y : y + 1, :] * values[y + 1]
            if x + 1 < layers:
                image = image - coef[x, 1, y : y + 1, :] * turned[(x + 1) % 2, y]
            high, low = split_two(image)
            left[:, y * nz : (y + 1) * nz] = value.astype(BF16)
            right[0:funcs, y * nz : (y + 1) * nz] = high
            right[funcs : 2 * funcs, y * nz : (y + 1) * nz] = low
        product = dot(right[...], left[...], NT)
        total = product if total is None else total + product

    @pl.when(comp == 0)
    def _():
        acc[...] = total

    @pl.when(comp > 0)
    def _():
        acc[...] += total

    @pl.when(comp == pl.num_programs(1) - 1)
    def _():
        out_ref[0] = acc[0:funcs] + acc[funcs : 2 * funcs]


def interior(edge, table, ids, basis, token):
    subs, funcs, comps, layers, ny, nz = basis.shape
    return pl.pallas_call(
        interior_kernel,
        grid=(subs, comps),
        in_specs=[SMEM, SMEM, VMEM, VMEM, ANY],
        out_specs=pl.BlockSpec((1, funcs, funcs), lambda s, c: (s, 0, 0)),
        out_shape=jax.ShapeDtypeStruct((subs, funcs, funcs), F32),
        scratch_shapes=[
            pltpu.VMEM((layers, funcs * ny, nz), F32),
            pltpu.VMEM((2, ny, funcs, nz), F32),
            pltpu.VMEM((layers, 4, ny, nz), F32),
            pltpu.VMEM((funcs, ny * nz), BF16),
            pltpu.VMEM((2 * funcs, ny * nz), BF16),
            pltpu.VMEM((2 * funcs, funcs), F32),
        ],
        compiler_params=pltpu.CompilerParams(vmem_limit_bytes=16 * 2**20),
        cost_estimate=LIGHT,
        name="interior",
    )(edge, table, ids, basis, token)


def face_kernel(flags_ref, table_ref, ids_ref, last_ref, halo_ref, token_ref, inner_ref, out_ref, *scratch):
    @pl.when(flags_ref[0] == 1)
    def _():
        last, halo, sems = scratch[-3:]
        copies = [
            pltpu.make_async_copy(last_ref, last, sems.at[0]),
            pltpu.make_async_copy(halo_ref, halo, sems.at[1]),
        ]
        for copy in copies:
            copy.start()
        for copy in copies:
            copy.wait()
        face_sums(table_ref, ids_ref, last, halo, inner_ref, out_ref, *scratch[:-3])


def face_sums(table_ref, ids_ref, last_ref, halo_ref, inner_ref, out_ref, mine, theirs, left, right, weights, acc):
    subs, layers, ny, nz = ids_ref.shape
    funcs = inner_ref.shape[1]
    comps = last_ref.shape[1] // funcs

    @pl.loop(0, subs)
    def _(sub):
        shear, dilate = lame_of(ids_ref[sub, layers - 1], table_ref)
        weights[0] = 0.5 * (shear + halo_ref[sub, comps * funcs].astype(F32))
        weights[1] = 0.5 * (dilate + halo_ref[sub, comps * funcs + 1].astype(F32))

        @pl.loop(0, comps)
        def _(comp):
            weight = weights[0] + jnp.where(comp == 0, weights[0] + weights[1], 0.0)
            rows = pl.ds(comp * funcs, funcs)
            mine[...] = last_ref[sub, rows].astype(F32).reshape(funcs * ny, nz)
            theirs[...] = halo_ref[sub, rows].astype(F32).reshape(funcs * ny, nz)
            for y in range(ny):
                here = mine[pl.ds(y, funcs, stride=ny), :]
                there = theirs[pl.ds(y, funcs, stride=ny), :]
                high, low = split_two(weight[y : y + 1, :] * (here - there))
                left[0:funcs, y * nz : (y + 1) * nz] = here.astype(BF16)
                left[funcs : 2 * funcs, y * nz : (y + 1) * nz] = there.astype(BF16)
                right[0:funcs, y * nz : (y + 1) * nz] = high
                right[funcs : 2 * funcs, y * nz : (y + 1) * nz] = low
            product = dot(right[...], left[...], NT)

            @pl.when(comp == 0)
            def _():
                acc[...] = product

            @pl.when(comp > 0)
            def _():
                acc[...] += product

        total = acc[:, 0:funcs] - acc[:, funcs : 2 * funcs]
        half = inner_ref[sub] + 0.5 * (total[0:funcs] + total[funcs : 2 * funcs])
        out_ref[sub] = half + half.T


def face(flags, table, ids, last, halo, token, inner):
    subs, layers, ny, nz = ids.shape
    funcs = inner.shape[1]
    return pl.pallas_call(
        face_kernel,
        in_specs=[SMEM, SMEM, VMEM, ANY, ANY, ANY, VMEM],
        out_specs=VMEM,
        out_shape=jax.ShapeDtypeStruct((subs, funcs, funcs), F32),
        scratch_shapes=[
            pltpu.VMEM((funcs * ny, nz), F32),
            pltpu.VMEM((funcs * ny, nz), F32),
            pltpu.VMEM((2 * funcs, ny * nz), BF16),
            pltpu.VMEM((2 * funcs, ny * nz), BF16),
            pltpu.VMEM((2, ny, nz), F32),
            pltpu.VMEM((2 * funcs, 2 * funcs), F32),
            pltpu.VMEM(last.shape, BF16),
            pltpu.VMEM(halo.shape, BF16),
            pltpu.SemaphoreType.DMA((2,)),
        ],
        compiler_params=pltpu.CompilerParams(vmem_limit_bytes=16 * 2**20),
        cost_estimate=LIGHT,
        name="face",
    )(flags, table, ids, last, halo, token, inner)


def spread(gal_ref, column_ids_ref, row_ids_ref, size):
    subs, funcs = column_ids_ref.shape[0:2]
    added = jnp.zeros((size, size), F32)
    lane = lax.broadcasted_iota(jnp.int32, (funcs, size), 1)
    row = lax.broadcasted_iota(jnp.int32, (size, funcs), 0)
    for sub in range(subs):
        slots = (column_ids_ref[sub] == lane).astype(F32)
        slots_t = (row_ids_ref[sub] == row).astype(F32)
        added = added + exact_dot(slots_t, exact_dot(gal_ref[sub], slots))
    return added


def assemble_kernel(flags_ref, token_ref, column_ids_ref, row_ids_ref, slab_ref, head_ref, *rest):
    gal_refs, (message_ref, sum_ref) = rest[:-2], rest[-2:]
    size = message_ref.shape[0]
    mode, own = flags_ref[0], flags_ref[1]
    message_ref[...] = jnp.zeros_like(message_ref)

    @pl.when((mode == 1) & (own == 1))
    def _():
        total = gal_refs[0][...]
        for gal_ref in gal_refs[1:]:
            total = total + gal_ref[...]
        sum_ref[...] = total
        added = spread(sum_ref, column_ids_ref, row_ids_ref, size)
        message_ref[...] = added + slab_ref[...].astype(F32)

    @pl.when((mode == 2) & (own == 1))
    def _():
        message_ref[...] = head_ref[...].astype(F32)


def assemble(flags, token, ids, slab, head, parts):
    size = slab.shape[1]
    block = pl.BlockSpec((size, size), lambda i: (0, 0))
    return pl.pallas_call(
        assemble_kernel,
        grid=(1,),
        in_specs=[SMEM, ANY, VMEM, VMEM, block, block] + [VMEM] * len(parts),
        out_specs=VMEM,
        out_shape=jax.ShapeDtypeStruct((size, size), F32),
        scratch_shapes=[pltpu.VMEM(parts[0].shape, F32)],
        cost_estimate=LIGHT,
        name="assemble",
    )(flags, token, ids[:, :, None], ids[:, None, :], slab, head, *parts)


def factor_kernel(flags_ref, token_ref, *refs, parts, groups):
    message_refs, gal_refs = refs[:parts], refs[parts:-4]
    summary_ref, block_ref, sum_ref, work = refs[-4:]
    subs, funcs = gal_refs[0].shape[0:2]
    size = summary_ref.shape[1]
    diagonal = message_refs[0][...]
    for message_ref in message_refs[1:]:
        diagonal = diagonal + message_ref[...]
    block_ref[...] = diagonal

    @pl.when(flags_ref[0] == 1)
    def _():
        row = lax.broadcasted_iota(jnp.int32, (size, size), 0)
        lane = lax.broadcasted_iota(jnp.int32, (size, size), 1)
        work[:, 0:size] = 0.5 * (diagonal + diagonal.T)
        work[:, size : 2 * size] = (row == lane).astype(F32)
        index = lax.broadcasted_iota(jnp.int32, (BLOCK, size), 0)
        for start in range(0, size, BLOCK):
            panel = work[start : start + BLOCK, 0:size]
            extra = work[start : start + BLOCK, size : 2 * size]
            columns = [
                jnp.broadcast_to(panel[:, start + step : start + step + 1], (BLOCK, size))
                for step in range(BLOCK)
            ]
            for step in range(BLOCK):
                scale = lax.rsqrt(columns[step][step : step + 1, :])
                column = jnp.where(index > step, columns[step] * scale, 0.0)
                for later in range(step + 1, BLOCK):
                    columns[later] = columns[later] - column * column[later : later + 1, :]
                pivot = panel[step : step + 1, :] * scale
                panel = jnp.where(index == step, pivot, panel - column * pivot)
                pivot = extra[step : step + 1, :] * scale
                extra = jnp.where(index == step, pivot, extra - column * pivot)
            work[start : start + BLOCK, 0:size] = panel
            work[start : start + BLOCK, size : 2 * size] = extra
            rest = start + BLOCK
            if rest < size:
                both = jnp.concatenate([panel, extra], axis=1)
                work[rest:size, :] -= exact_dot(panel[:, rest:size], both, TN)
        upper = jnp.where(row <= lane, work[:, 0:size], 0.0)
        inverse = jnp.where(row >= lane, work[:, size : 2 * size], 0.0).T
        high = inverse.astype(BF16)
        summary_ref[0:size] = high
        summary_ref[size : 2 * size] = (inverse - high.astype(F32)).astype(BF16)
        summary_ref[2 * size : 3 * size] = upper.T.astype(BF16)
        each = len(gal_refs) // groups
        for group in range(groups):

            @pl.when(flags_ref[1] == group)
            def _(chosen=gal_refs[group * each : (group + 1) * each]):
                total = chosen[0][...]
                for gal_ref in chosen[1:]:
                    total = total + gal_ref[...]
                sum_ref[...] = total


def factorize(flags, token, messages, groups):
    size = messages[0].shape[1]
    subs, funcs = groups[0][0].shape[0:2]
    parts = [part for group in groups for part in group]
    return pl.pallas_call(
        functools.partial(factor_kernel, parts=len(messages), groups=len(groups)),
        in_specs=[SMEM, ANY] + [VMEM] * (len(messages) + len(parts)),
        out_specs=[VMEM] * 3,
        out_shape=[
            jax.ShapeDtypeStruct((3 * size, size), BF16),
            jax.ShapeDtypeStruct((size, size), F32),
            jax.ShapeDtypeStruct(groups[0][0].shape, F32),
        ],
        scratch_shapes=[pltpu.VMEM((size, 2 * size), F32)],
        cost_estimate=LIGHT,
        name="factorize",
    )(flags, token, *messages, *parts)


def prepare_kernel(flags_ref, token_ref, head_ref, *rest, sources):
    summary_refs = rest[:sources]
    weights_ref, rows_ref, lower_ref, summary, sem = rest[sources:]
    size = head_ref.shape[0]
    choice, mode = flags_ref[0], flags_ref[1]
    for number, summary_ref in enumerate(summary_refs):

        @pl.when(choice == number)
        def _(summary_ref=summary_ref):
            copy = pltpu.make_async_copy(summary_ref, summary, sem)
            copy.start()
            copy.wait()

    def doubled(block):
        nothing = jnp.zeros((size, size), BF16)
        top = jnp.concatenate([block, nothing], axis=1)
        return jnp.concatenate([top, jnp.concatenate([nothing, block], axis=1)], axis=0)

    @pl.when(mode > 0)
    def _():
        weights_ref[0 : 2 * size] = doubled(summary[0:size])
        weights_ref[2 * size : 4 * size] = doubled(summary[size : 2 * size])
        lower_ref[...] = summary[2 * size : 3 * size]

    @pl.when(mode == 2)
    def _():
        inverse = summary[0:size].astype(F32) + summary[size : 2 * size].astype(F32)
        solved = exact_dot(head_ref[...], inverse)
        rows_ref[...] = doubled(solved.T.astype(BF16))


def prepare(flags, token, head, summaries):
    size = head.shape[0]
    return pl.pallas_call(
        functools.partial(prepare_kernel, sources=len(summaries)),
        in_specs=[SMEM, ANY, VMEM] + [ANY] * len(summaries),
        out_specs=[VMEM] * 3,
        out_shape=[
            jax.ShapeDtypeStruct((4 * size, 2 * size), BF16),
            jax.ShapeDtypeStruct((2 * size, 2 * size), BF16),
            jax.ShapeDtypeStruct((size, size), BF16),
        ],
        scratch_shapes=[pltpu.VMEM(summaries[0].shape, BF16), pltpu.SemaphoreType.DMA],
        compiler_params=pltpu.CompilerParams(vmem_limit_bytes=16 * 2**20),
        cost_estimate=LIGHT,
        name="prepare",
    )(flags, token, head, *summaries)


def added_kernel(flags_ref, token_ref, column_ids_ref, row_ids_ref, sum_ref, added_ref):
    @pl.when(flags_ref[0] == 1)
    def _():
        added_ref[...] = spread(sum_ref, column_ids_ref, row_ids_ref, added_ref.shape[0])


def added_of(flags, token, ids, galerkin, size):
    return pl.pallas_call(
        added_kernel,
        in_specs=[SMEM, ANY, VMEM, VMEM, VMEM],
        out_specs=VMEM,
        out_shape=jax.ShapeDtypeStruct((size, size), F32),
        cost_estimate=LIGHT,
        name="added",
    )(flags, token, ids[:, :, None], ids[:, None, :], galerkin)


def panel_kernel(
    flags_ref, token_ref, lower_ref, weights_ref, rows_ref, added_ref, slab_ref, *rest, pieces, spans, first
):
    hops = len(pieces) // len(spans)
    others = rest[: len(pieces)]
    out_ref, done_ref, column, factor, sems = rest[-5:]
    done_ref[0] = flags_ref[0]
    tile, size = out_ref.shape
    half = tile // 2
    mode, head, own, which = flags_ref[0], flags_ref[1], flags_ref[2], flags_ref[3]
    step, steps = pl.program_id(0), pl.num_programs(0)
    top = first & (step == 0)

    def copy_of(at, act):
        for number, (begin, end) in enumerate(spans):
            for hop in range(hops):

                @pl.when((mode == 2) & (which == hop) & (at >= begin) & (at < end))
                def _(other_ref=others[number * hops + hop], begin=begin):
                    source = other_ref.at[pl.ds(pl.multiple_of((at - begin) * tile, tile), tile)]
                    act(pltpu.make_async_copy(source, column.at[at % 2], sems.at[at % 2]))

    @pl.when(step == 0)
    def _():
        copy_of(step, lambda copy: copy.start())

    @pl.when(step + 1 < steps)
    def _():
        copy_of(step + 1, lambda copy: copy.start())

    @pl.when(mode == 0)
    def _():
        out_ref[...] = slab_ref[...]

    @pl.when(mode == 1)
    def _():
        column[step % 2] = slab_ref[...]

    @pl.when(mode == 2)
    def _():
        copy_of(step, lambda copy: copy.wait())

    @pl.when(mode > 0)
    def _():
        value = column[step % 2]
        pair = jnp.concatenate([value[0:half], value[half:tile]], axis=1)
        factor[...] = dot(jnp.concatenate([pair, pair], axis=1), weights_ref[...]).astype(BF16)

        @pl.when(top & (head == 1))
        def _():
            factor[0:size, 0:size] = lower_ref[...]

        @pl.when(top & (head == 2))
        def _():
            factor[0:size, 0:size] = jnp.zeros((size, size), BF16)

    @pl.when(mode == 1)
    def _():
        out_ref[0:half] = factor[:, 0:size]
        out_ref[half:tile] = factor[:, size : 2 * size]

    @pl.when(mode == 2)
    def _():
        update = dot(factor[...], rows_ref[...])
        out_ref[0:half] = (slab_ref[0:half].astype(F32) - update[:, 0:size]).astype(BF16)
        out_ref[half:tile] = (slab_ref[half:tile].astype(F32) - update[:, size : 2 * size]).astype(BF16)

        @pl.when(top & (own == 1))
        def _():
            base = slab_ref[0:size].astype(F32) + added_ref[...]
            out_ref[0:size] = (base - update[0:size, 0:size]).astype(BF16)


def panel(flags, token, lower, weights, rows, added, slab, parts, old, start, tile):
    size = slab.shape[1]
    offset = start // tile
    spans, begin, operands = [], 0, []
    for hops in parts:
        end = begin + hops[0].shape[0] // tile
        spans.append((begin, end))
        begin = end
        operands += hops
    blocks = [
        SMEM,
        ANY,
        pl.BlockSpec((size, size), lambda i: (0, 0)),
        pl.BlockSpec(weights.shape, lambda i: (0, 0)),
        pl.BlockSpec(rows.shape, lambda i: (0, 0)),
        pl.BlockSpec((size, size), lambda i: (0, 0)),
        pl.BlockSpec((tile, size), lambda i: (i + offset, 0)),
    ] + [ANY] * len(operands)
    pieces = len(operands)
    operands = [flags, token, lower, weights, rows, added, slab] + operands
    aliases = {}
    if old is not None:
        aliases = {len(operands): 0}
        blocks.append(ANY)
        operands.append(old)
    return pl.pallas_call(
        functools.partial(panel_kernel, pieces=range(pieces), spans=spans, first=start == 0),
        grid=(begin,),
        in_specs=blocks,
        out_specs=[pl.BlockSpec((tile, size), lambda i: (i + offset, 0)), SMEM],
        out_shape=[jax.ShapeDtypeStruct(slab.shape, BF16), jax.ShapeDtypeStruct((1,), jnp.int32)],
        input_output_aliases=aliases,
        scratch_shapes=[
            pltpu.VMEM((2, tile, size), BF16),
            pltpu.VMEM((tile // 2, 2 * size), BF16),
            pltpu.SemaphoreType.DMA((2,)),
        ],
        compiler_params=pltpu.CompilerParams(vmem_limit_bytes=16 * 2**20),
        cost_estimate=LIGHT,
        name="panel",
    )(*operands)


def broadcast(value, axis, source):
    kept = jnp.where(lax.axis_index(axis) == source, value, 0).astype(value.dtype)
    return lax.psum(kept, axis)


def settings(*values):
    return jnp.stack([jnp.asarray(value).astype(jnp.int32) for value in values])


def holder_pairs(wide, narrow, distance):
    stride = wide // narrow
    found = []
    for n in range(narrow):
        for start in range(0, wide, 2 * distance):
            source = (n * stride) ^ start
            found.append((source * narrow + n, (source ^ distance) * narrow + n))
    return found


class Order:
    def __init__(self, token):
        self.token = token

    def after(self, value):
        value, self.token = lax.optimization_barrier((value, self.token))
        return value


def known_owner(owner, coarse_basis, material_ids, lame_table, coarse_ids, coarse_slab):
    narrow, wide = lax.axis_size("narrow"), lax.axis_size("wide")
    stride = wide // narrow
    wide_index, narrow_index = lax.axis_index("wide"), lax.axis_index("narrow")
    height, block = coarse_slab.shape
    own = wide_index == narrow_index * stride
    later = narrow_index > owner
    which = jnp.where(later, narrow_index - owner - 1, -1)
    mode = jnp.where(narrow_index == owner, 1, jnp.where(later, 2, 0))
    earlier = (wide_index % stride == 0) & (wide_index // stride < owner)
    kind = jnp.where(wide_index == owner * stride, 1, jnp.where(earlier, 2, 0))
    table = lame_table.astype(F32)
    hops = narrow - 1 - owner
    units, joined, waits, plan = PLANS[hops]
    unit = height // sum(units)
    count = len(units)
    bounds, low = [], 0
    for number in units:
        bounds.append((low, low + number * unit))
        low += number * unit
    axes = ("wide", "narrow")

    def rows_of(number):
        low, high = bounds[number]
        return coarse_slab[low:high]

    def send(value, source, target):
        return lax.ppermute(value, "narrow", [(owner + source, owner + target)])

    order = Order(settings(mode))

    holders = [((n * stride) * narrow + owner, (n * stride) * narrow + n) for n in range(owner + 1, narrow)]
    moved = {}

    groups = [[w for w in range(wide) if w % stride == 0], [w for w in range(wide) if w % stride]]
    groups = [group for group in groups if group]
    member = jnp.where(wide_index % stride == 0, 0, 1)

    def within(group, pairs):
        return [(w * narrow + one, w * narrow + two) for w in group for one, two in pairs]

    def halo_of(group, message):
        return lax.ppermute(message, axes, within(group, [(i + 1, i) for i in range(narrow - 1)]))

    spans = [bounds[0], (bounds[1][0], height) if joined else bounds[1]]
    first, last, *begun = halo_message(table, material_ids, order.token, coarse_basis, coarse_slab, spans)
    first = order.after(first)
    halos = [halo_of(groups[0], first)]
    edge = (narrow_index == 0).astype(jnp.int32).reshape(1)
    inner = order.after(interior(edge, table, material_ids, coarse_basis, order.token))
    head = order.after(lax.ppermute(order.after(coarse_slab[:block]), axes, holders))
    halos[0] = order.after(halos[0])
    moved[0] = [send(order.after(begun[0]), 0, hops)]
    for group in groups[1:]:
        halos.append(halo_of(group, order.after(first)))

    def nearest(base, extent):
        return min(range(base, min(base + extent, narrow)), key=lambda n: abs(n - owner))

    def summed(parts, distance, group):
        total = parts[0] if len(parts) == 1 else parts[0] + parts[1]
        pairs = []
        for base in range(0, narrow - distance, 2 * distance):
            one, two = nearest(base, distance), nearest(base + distance, distance)
            pairs.append((two, one) if nearest(base, 2 * distance) == one else (one, two))
        return [total, lax.ppermute(total, axes, within(group, pairs))], 2 * distance

    def faces_of(number):
        flag = settings(member == number)
        return [order.after(face(flag, table, material_ids, last, halos[number], order.token, inner))]

    sums, reach = [faces_of(0)], [1]
    while reach[0] < narrow:
        sums[0], reach[0] = summed(sums[0], reach[0], groups[0])
    sums[0][1] = order.after(sums[0][1])
    distance, messages, left = wide // 2, [], plan.count("spread")
    result, prepared = None, None
    choice = (narrow_index - owner) % narrow
    flags = settings(mode, kind, own, which)
    for step in plan:
        if step[0] == "panel":
            if prepared is None:
                prepared = prepare(settings(choice, mode), order.token, head, summaries)
            weights, rows, lower = prepared
            begin, end = step[1:]
            parts = [moved[number][:: 1 if number else -1] for number in range(begin, end)]
            result, order.token = panel(
                flags, order.token, lower, weights, rows, added if begin == 0 else head, coarse_slab, parts, result, bounds[begin][0], 2 * unit
            )
        elif step == "added":
            added = added_of(settings(mode), order.token, coarse_ids, galerkin, block)
            added = order.after(lax.ppermute(added, axes, holders))
            if waits:
                moved[count - 1] = [send(order.after(rows_of(count - 1)), 0, 1)]
        elif step == "sums":
            galerkins = [order.after(part) for part in galerkins]
            galerkin = jnp.where(narrow_index == owner, galerkin, sum(galerkins))
        elif step == "next":
            if joined:
                whole = send(order.after(begun[1]), 0, 1)
            else:
                moved[1] = [send(order.after(begun[1]), 0, 1)]
                for number in range(2, count - waits):
                    moved[number] = [send(order.after(rows_of(number)), 0, 1)]
        elif step == "assemble":
            message = assemble(settings(mode, own), order.token, coarse_ids, coarse_slab, head, sums[0])
            message = order.after(message)
        elif step == "others":
            for number in range(1, len(groups)):
                halos[number] = order.after(halos[number])
                parts, far = summed(faces_of(number), 1, groups[number])
                sums.append(parts)
                reach.append(far)
        elif step == "more":
            for number in range(1, len(groups)):
                while reach[number] < narrow:
                    sums[number][1] = order.after(sums[number][1])
                    sums[number], reach[number] = summed(sums[number], reach[number], groups[number])
        elif step == "spread":
            left -= 1
            while distance:
                received = order.after(lax.ppermute(message, axes, holder_pairs(wide, narrow, distance)))
                messages = [message, received]
                if distance > 1:
                    message = message + received
                distance //= 2
                if left:
                    break
        elif step == "factor":
            summary, head, galerkin = factorize(settings(mode, member), order.token, messages, sums)
            summary = order.after(summary)
            ways = [[(owner, (owner + place) % narrow)] for place in range(1, narrow)]
            summaries = [summary] + [lax.ppermute(summary, "narrow", way) for way in ways]
        elif step == "summary":
            for place in range(1, narrow):
                summaries[place] = order.after(summaries[place])
            galerkin = order.after(galerkin)
            galerkins = [lax.ppermute(galerkin, "narrow", way) for way in ways]
        else:
            number, hop = step
            if joined and step == (1, 0):
                whole = order.after(whole)
                for part in range(1, count):
                    low, high = (bound - bounds[1][0] for bound in bounds[part])
                    moved[part] = [whole[low:high]]
            moving = moved[number][hop] = order.after(moved[number][hop])
            if number == 0 and hop + 1 < hops:
                moved[number].append(send(moving, hops - hop, hops - hop - 1))
            elif number != 0 and hop + 1 < hops:
                moved[number].append(send(moving, hop + 1, hop + 2))
    return result, galerkin


def any_owner(owner, coarse_basis, material_ids, lame_table, coarse_ids, coarse_slab):
    narrow, wide = lax.axis_size("narrow"), lax.axis_size("wide")
    stride = wide // narrow
    wide_index, narrow_index = lax.axis_index("wide"), lax.axis_index("narrow")
    own = wide_index == narrow_index * stride
    later = narrow_index > owner
    which = jnp.where(later, 0, -1)
    mode = jnp.where(narrow_index == owner, 1, jnp.where(later, 2, 0))
    earlier = (wide_index % stride == 0) & (wide_index // stride < owner)
    kind = jnp.where(wide_index == owner * stride, 1, jnp.where(earlier, 2, 0))
    table = lame_table.astype(F32)
    column = broadcast(coarse_slab, "narrow", owner)
    first, last = halo_message(table, material_ids, table, coarse_basis, coarse_slab, ())
    halo = lax.ppermute(first, "narrow", [(i + 1, i) for i in range(narrow - 1)])
    edge = (narrow_index == 0).astype(jnp.int32).reshape(1)
    inner = interior(edge, table, material_ids, coarse_basis, first)
    partial = face(settings(1), table, material_ids, last, halo, first, inner)
    parts = [lax.psum(partial, "narrow")]
    message = assemble(settings(mode, own), first, coarse_ids, coarse_slab, column, parts)
    at_owner = (wide_index == owner * stride) & (narrow_index == owner)
    diagonal = lax.psum(jnp.where(at_owner, message, 0.0), ("wide", "narrow"))
    summary, _, galerkin = factorize(settings(1, 0), first, [diagonal], [parts])
    head = broadcast(message, "wide", narrow_index * stride)
    weights, rows, lower = prepare(settings(0, mode), settings(mode), head, [summary])
    added = added_of(settings(1), weights, coarse_ids, galerkin, head.shape[0])
    flags = settings(mode, kind, own, which)
    tile = coarse_slab.shape[0] // 12
    result, _ = panel(flags, flags, lower, weights, rows, added, coarse_slab, [[column]], None, 0, tile)
    return result, galerkin


def on_device(coarse_basis, material_ids, lame_table, coarse_ids, coarse_slab, panel_owner):
    narrow, wide = lax.axis_size("narrow"), lax.axis_size("wide")
    arrays = (coarse_basis, material_ids, lame_table, coarse_ids, coarse_slab)
    owner = panel_owner[0]
    if narrow - 1 > len(PLANS) or wide & (wide - 1):
        return any_owner(owner, *arrays)
    branches = [functools.partial(known_owner, place) for place in range(narrow - 1)]
    return lax.switch(owner, branches, *arrays)


def solution(mesh):
    return jax.shard_map(
        on_device,
        mesh=mesh,
        in_specs=(
            P("wide", None, None, "narrow", None, None),
            P("wide", "narrow", None, None),
            P(),
            P("wide", None),
            P("wide", "narrow"),
            P(),
        ),
        out_specs=(P("wide", "narrow"), P("wide", None, None)),
        check_vma=False,
    )
```

profile of v0, /device:TPU:22, one launch (start us, length us, event | category | flops | bytes accessed | tf_op | source)
XLA Modules:
  0.0 136.4 jit_solution(11689639104472071585)
XLA Ops:
  1.3 135.1 %conditional.1 = (bf16[12288,128]{1,0:T(8,128)(2,1)}, f32[2,96,96]{2,1,0:T(8,128)}) conditional(s32[]{:T(128)} %bitcast.33, (bf16[2,16]{1,0:T(2,128)(2,1)}, s32[2,4,8,128]{3,2,1,0:T(8,128)}, bf16[2,96,3,4,8,128]{5,4,3,2,1,0:T(8,128)(2,1)}, bf16[12288,128]{1,0:T(8,128)(2,1)}, s32[2,96]{1,0:T(2,128)}) %tuple.112, ...), branch_computations={%region_0.1_spmd, %region_1.2_spmd, %region_2.3_spmd} | conditional | flops 125047 | bytes 95779632 | solution.py:813
  2.0 5.5 %halo_message.4 = (bf16[2,290,8,128]{3,2,1,0:T(8,128)(2,1)}, bf16[2,288,8,128]{3,2,1,0:T(8,128)(2,1)S(1)}, bf16[6144,128]{1,0:T(8,128)(2,1)}, bf16[3072,128]{1,0:T(8,128)(2,1)S(1)}) custom-call(f32[2,16]{1,0:T(2,128)S(1)} %convert_element_type.2.table_ref, s32[2,4,8,128]{3,2,1,0:T(8,128)} %get-tuple-element.117.ids_ref, s32[1]{0:T(128)} %bitcast.11.token_ref.flags_ref, ...), custom_call_target="tpu_custom_call" | custom-call | flops 1 | bytes 1 | tf_op jit(solution)/shard_map/cond/branch_1_fun/halo_message/pallas_call | solution.py:94
  7.5 0.9 copy-done.14
  8.4 2.5 %collective-permute-start.26 = (bf16[2,290,8,128]{3,2,1,0:T(8,128)(2,1)}, bf16[2,290,8,128]{3,2,1,0:T(8,128)(2,1)S(1)}, u32[]{:S(2)}, u32[]{:S(2)}) collective-permute-start(bf16[2,290,8,128]{3,2,1,0:T(8,128)(2,1)} %get-tuple-element.148), channel_id=1, source_target_pairs={{1,0},{2,1},{3,2},{9,8},{10,9},{11,10},{17,16},{18,17},{19,18},{25... | collective-permute-start | bytes 3563528 | tf_op jit(solution)/shard_map/cond/branch_1_fun/ppermute | solution.py:664
  11.0 10.7 %interior.4.inner_ref = f32[2,96,96]{2,1,0:T(8,128)S(1)} custom-call(s32[1]{0:T(128)} %bitcast.17.edge_ref, f32[2,16]{1,0:T(2,128)S(1)} %convert_element_type.2.table_ref, s32[2,4,8,128]{3,2,1,0:T(8,128)S(1)} %copy-done.22, bf16[2,96,3,4,8,128]{5,4,3,2,1,0:T(8,128)(2,1)} %get-tuple-element.118.basis_ref, s32[1]{0:T(128)} %bitcast.11.token_ref.flags_ref), custom_call_target="tpu_custom_call" | custom-call | flops 1 | bytes 1 | tf_op jit(solution)/shard_map/cond/branch_1_fun/interior/pallas_call | solution.py:190
  21.7 0.8 slice.16
  23.1 3.6 %collective-permute-done.26.halo_ref = bf16[2,290,8,128]{3,2,1,0:T(8,128)(2,1)S(1)} collective-permute-done((bf16[2,290,8,128]{3,2,1,0:T(8,128)(2,1)}, bf16[2,290,8,128]{3,2,1,0:T(8,128)(2,1)S(1)}, u32[]{:S(2)}, u32[]{:S(2)}) %collective-permute-start.26) | collective-permute-done | bytes 1187872 | tf_op jit(solution)/shard_map/cond/branch_1_fun/ppermute | solution.py:664
  26.8 1.1 copy-done
  27.9 0.7 collective-permute-start.31
  28.6 1.7 %collective-permute-start.34 = (bf16[2,290,8,128]{3,2,1,0:T(8,128)(2,1)}, bf16[2,290,8,128]{3,2,1,0:T(8,128)(2,1)}, u32[]{:S(2)}, u32[]{:S(2)}) collective-permute-start(bf16[2,290,8,128]{3,2,1,0:T(8,128)(2,1)} %get-tuple-element.148), channel_id=1, source_target_pairs={{5,4},{6,5},{7,6},{13,12},{14,13},{15,14},{21,20},{22,21},{23,22},... | collective-permute-start | bytes 3563528 | tf_op jit(solution)/shard_map/cond/branch_1_fun/ppermute | solution.py:664
  30.3 1.3 copy-done.1
  31.6 4.5 %face.8 = f32[2,96,96]{2,1,0:T(8,128)S(1)} custom-call(s32[1]{0:T(128)} %bitcast.16.flags_ref, f32[2,16]{1,0:T(2,128)S(1)} %convert_element_type.2.table_ref, s32[2,4,8,128]{3,2,1,0:T(8,128)S(1)} %copy-done.22, bf16[2,288,8,128]{3,2,1,0:T(8,128)(2,1)S(1)} %get-tuple-element.121.last_ref, bf16[2,290,8,128]{3,2,1,0:T(8,128)(2,1)S(1)} %copy-done.1, ...), custom_call_target="tpu_custom_call" | custom-call | flops 1 | bytes 1 | tf_op jit(solution)/shard_map/cond/branch_1_fun/face/pallas_call | solution.py:268
  36.1 1.3 collective-permute-start.28
  37.4 0.8 copy.18.column_ids_ref
  38.1 6.7 %collective-permute-done.28 = f32[2,96,96]{2,1,0:T(8,128)S(1)} collective-permute-done((f32[2,96,96]{2,1,0:T(8,128)S(1)}, f32[2,96,96]{2,1,0:T(8,128)S(1)}, u32[]{:S(2)}, u32[]{:S(2)}) %collective-permute-start.28) | collective-permute-done | bytes 73760 | tf_op jit(solution)/shard_map/cond/branch_1_fun/ppermute | solution.py:687
  44.8 6.7 %collective-permute-start.29 = (f32[2,96,96]{2,1,0:T(8,128)S(1)}, f32[2,96,96]{2,1,0:T(8,128)S(1)}, u32[]{:S(2)}, u32[]{:S(2)}) collective-permute-start(f32[2,96,96]{2,1,0:T(8,128)S(1)} %add.73.rest_0_.refs_2_), channel_id=1, source_target_pairs={{2,1},{10,9},{18,17},{26,25}} | collective-permute-start | bytes 221192 | tf_op jit(solution)/shard_map/cond/branch_1_fun/ppermute | solution.py:687
  52.2 1.6 %collective-permute-done.29.rest_1_.refs_3_ = f32[2,96,96]{2,1,0:T(8,128)S(1)} collective-permute-done((f32[2,96,96]{2,1,0:T(8,128)S(1)}, f32[2,96,96]{2,1,0:T(8,128)S(1)}, u32[]{:S(2)}, u32[]{:S(2)}) %collective-permute-start.29) | collective-permute-done | bytes 73760 | tf_op jit(solution)/shard_map/cond/branch_1_fun/ppermute | solution.py:687
  54.4 1.7 %assemble.4 = f32[128,128]{1,0:T(8,128)} custom-call(s32[2]{0:T(128)} %pad_add_fusion.6.flags_ref, s32[1]{0:T(128)} %bitcast.11.token_ref.flags_ref, s32[2,96,1]{2,1,0:T(8,128)} %copy.18.column_ids_ref, s32[2,1,96]{2,1,0:T(1,128)S(1)} %bitcast.38, bf16[12288,128]{1,0:T(8,128)(2,1)} %get-tuple-element.119.slab_ref, bf16[128,128]{1,0:T(8,128)(2,1)} %copy-done.50, ...), custom_call_target="tpu_custom_call" | custom-call | flops 1 | bytes 1 | tf_op jit(solution)/shard_map/cond/branch_1_fun/assemble/pallas_call | solution.py:325
  56.7 1.9 %slice.17 = bf16[2048,128]{1,0:T(8,128)(2,1)} slice(bf16[12288,128]{1,0:T(8,128)(2,1)} %get-tuple-element.119.slab_ref), slice={[9216:11264], [0:128]} | slice | bytes 1048576 | tf_op jit(solution)/shard_map/cond/branch_1_fun/slice | solution.py:646
  58.6 0.9 add.74
  59.5 1.3 collective-permute-start.33
  60.8 1.3 collective-permute-start.30
  63.3 2.3 %collective-permute-done.33 = f32[128,128]{1,0:T(8,128)S(1)} collective-permute-done((f32[128,128]{1,0:T(8,128)S(1)}, f32[128,128]{1,0:T(8,128)S(1)}, u32[]{:S(2)}, u32[]{:S(2)}) %collective-permute-start.33) | collective-permute-done | bytes 65568 | tf_op jit(solution)/shard_map/cond/branch_1_fun/ppermute | solution.py:743
  65.6 1.3 collective-permute-start.35
  67.0 0.9 collective-permute-done.35.refs_1_
  67.8 1.3 collective-permute-start.48
  69.1 1.3 collective-permute-start.41
  70.4 10.5 %collective-permute-done.30.rest_0_ = bf16[3072,128]{1,0:T(8,128)(2,1)} collective-permute-done((bf16[3072,128]{1,0:T(8,128)(2,1)}, bf16[3072,128]{1,0:T(8,128)(2,1)}, u32[]{:S(2)}, u32[]{:S(2)}) %collective-permute-start.30) | collective-permute-done | bytes 786464 | tf_op jit(solution)/shard_map/cond/branch_1_fun/ppermute | solution.py:649
  81.0 1.3 collective-permute-start.47
  84.2 1.8 %factorize.4 = (bf16[384,128]{1,0:T(8,128)(2,1)}, f32[128,128]{1,0:T(8,128)}, f32[2,96,96]{2,1,0:T(8,128)}) custom-call(s32[2]{0:T(128)} %pad_add_fusion.5.flags_ref, s32[1]{0:T(128)} %bitcast.11.token_ref.flags_ref, f32[128,128]{1,0:T(8,128)} %copy-done.38, f32[128,128]{1,0:T(8,128)} %copy-done.47, f32[2,96,96]{2,1,0:T(8,128)} %copy-done.25, ...), custom_call_target="tpu_custom_call" | custom-call | flops 1 | bytes 1 | tf_op jit(solution)/shard_map/cond/branch_1_fun/factorize/pallas_call | solution.py:397
  86.0 1.3 collective-permute-start.40
  88.0 2.3 %collective-permute-done.41.rest_0_ = bf16[2048,128]{1,0:T(8,128)(2,1)S(1)} collective-permute-done((bf16[2048,128]{1,0:T(8,128)(2,1)}, bf16[2048,128]{1,0:T(8,128)(2,1)S(1)}, u32[]{:S(2)}, u32[]{:S(2)}) %collective-permute-start.41) | collective-permute-done | bytes 524320 | tf_op jit(solution)/shard_map/cond/branch_1_fun/ppermute | solution.py:649
  90.9 3.6 %collective-permute-done.40.rest_1_ = bf16[384,128]{1,0:T(8,128)(2,1)S(1)} collective-permute-done((bf16[384,128]{1,0:T(8,128)(2,1)}, bf16[384,128]{1,0:T(8,128)(2,1)S(1)}, u32[]{:S(2)}, u32[]{:S(2)}) %collective-permute-start.40) | collective-permute-done | bytes 98336 | tf_op jit(solution)/shard_map/cond/branch_1_fun/ppermute | solution.py:754
  94.6 1.6 %added.4 = f32[128,128]{1,0:T(8,128)} custom-call(s32[1]{0:T(128)} %bitcast.11.token_ref.flags_ref, s32[1]{0:T(128)} %bitcast.11.token_ref.flags_ref, s32[2,96,1]{2,1,0:T(8,128)} %copy.18.column_ids_ref, s32[2,1,96]{2,1,0:T(1,128)S(1)} %bitcast.39, f32[2,96,96]{2,1,0:T(8,128)} %get-tuple-element.171.sum_ref), custom_call_target="tpu_custom_call" | custom-call | flops 1 | bytes 1 | tf_op jit(solution)/shard_map/cond/branch_1_fun/added/pallas_call | solution.py:468
  96.8 1.7 %slice.18 = bf16[1024,128]{1,0:T(8,128)(2,1)} slice(bf16[12288,128]{1,0:T(8,128)(2,1)} %get-tuple-element.119.slab_ref), slice={[11264:12288], [0:128]} | slice | bytes 524288 | tf_op jit(solution)/shard_map/cond/branch_1_fun/slice | solution.py:646
  98.5 1.3 collective-permute-start.46
  99.7 10.6 %collective-permute-start.49 = (bf16[2048,128]{1,0:T(8,128)(2,1)S(1)}, bf16[2048,128]{1,0:T(8,128)(2,1)}, u32[]{:S(2)}, u32[]{:S(2)}) collective-permute-start(bf16[2048,128]{1,0:T(8,128)(2,1)S(1)} %collective-permute-done.41.rest_0_), channel_id=1, source_target_pairs={{2,3},{6,7},{10,11},{14,15},{18,19},{22,23},{26,27},{30,31}} | collective-permute-start | bytes 1572872 | tf_op jit(solution)/shard_map/cond/branch_1_fun/ppermute | solution.py:649
  110.4 1.3 collective-permute-start.44
  111.7 1.4 %collective-permute-done.46.rest_2_ = bf16[1024,128]{1,0:T(8,128)(2,1)S(1)} collective-permute-done((bf16[1024,128]{1,0:T(8,128)(2,1)}, bf16[1024,128]{1,0:T(8,128)(2,1)S(1)}, u32[]{:S(2)}, u32[]{:S(2)}) %collective-permute-start.46) | collective-permute-done | bytes 262176 | tf_op jit(solution)/shard_map/cond/branch_1_fun/ppermute | solution.py:649
  113.7 0.7 collective-permute-start.42
  114.5 0.8 copy-done.7
  115.3 0.9 copy-done.10
  116.2 1.0 prepare.4
  117.3 4.8 %panel.11 = (bf16[12288,128]{1,0:T(8,128)(2,1)S(1)}, s32[1]{0:T(128)}) custom-call(s32[4]{0:T(128)S(1)} %pad_add_fusion.4.flags_ref, s32[1]{0:T(128)} %bitcast.11.token_ref.flags_ref, bf16[128,128]{1,0:T(8,128)(2,1)S(1)} %get-tuple-element.180.lower_ref, bf16[512,256]{1,0:T(8,128)(2,1)S(1)} %get-tuple-element.181.weights_ref, ...), custom_call_target="tpu_custom_call" | custom-call | flops 1 | bytes 1 | tf_op jit(solution)/shard_map/cond/branch_1_fun/panel/pallas_call | solution.py:576
  122.0 1.3 collective-permute-start.50
  123.4 7.0 %panel.12 = (bf16[12288,128]{1,0:T(8,128)(2,1)S(1)}, s32[1]{0:T(128)}) custom-call(s32[4]{0:T(128)S(1)} %pad_add_fusion.4.flags_ref, s32[1]{0:T(128)} %get-tuple-element.185.token_ref, bf16[128,128]{1,0:T(8,128)(2,1)S(1)} %get-tuple-element.180.lower_ref, bf16[512,256]{1,0:T(8,128)(2,1)S(1)} %get-tuple-element.181.weights_ref, ...), custom_call_target="tpu_custom_call", output_to_operand_aliasing={{0}: (9, {})} | custom-call | flops 1 | bytes 1 | tf_op jit(solution)/shard_map/cond/branch_1_fun/panel/pallas_call | solution.py:576
  131.1 3.6 %panel.13 = (bf16[12288,128]{1,0:T(8,128)(2,1)S(1)}, s32[1]{0:T(128)}) custom-call(s32[4]{0:T(128)S(1)} %pad_add_fusion.4.flags_ref, s32[1]{0:T(128)} %get-tuple-element.192.token_ref, bf16[128,128]{1,0:T(8,128)(2,1)S(1)} %get-tuple-element.180.lower_ref, bf16[512,256]{1,0:T(8,128)(2,1)S(1)} %get-tuple-element.181.weights_ref, ...), custom_call_target="tpu_custom_call", output_to_operand_aliasing={{0}: (11, {})} | custom-call | flops 1 | bytes 1 | tf_op jit(solution)/shard_map/cond/branch_1_fun/panel/pallas_call | solution.py:576
  134.7 1.7 %copy-done.19 = bf16[12288,128]{1,0:T(8,128)(2,1)} copy-done((bf16[12288,128]{1,0:T(8,128)(2,1)}, bf16[12288,128]{1,0:T(8,128)(2,1)S(1)}, u32[]{:S(2)}) %copy-start.19) | copy-done | bytes 3145752 | tf_op jit(solution)/shard_map/cond
  (62 shorter events, 9.9 us)
Async XLA Ops:
  2.0 9.0 %copy-start.22 = (s32[2,4,8,128]{3,2,1,0:T(8,128)S(1)}, s32[2,4,8,128]{3,2,1,0:T(8,128)}, u32[]{:S(2)}) copy-start(s32[2,4,8,128]{3,2,1,0:T(8,128)} %get-tuple-element.117.ids_ref) | copy-start | bytes 98308 | tf_op jit(solution)/shard_map/cond
  7.5 0.9 copy-start.14
  8.4 18.4 %collective-permute-start.26 = (bf16[2,290,8,128]{3,2,1,0:T(8,128)(2,1)}, bf16[2,290,8,128]{3,2,1,0:T(8,128)(2,1)S(1)}, u32[]{:S(2)}, u32[]{:S(2)}) collective-permute-start(bf16[2,290,8,128]{3,2,1,0:T(8,128)(2,1)} %get-tuple-element.148), channel_id=1, source_target_pairs={{1,0},{2,1},{3,2},{9,8},{10,9},{11,10},{17,16},{18,17},{19,18},{25... | collective-permute-start | bytes 3563528 | tf_op jit(solution)/shard_map/cond/branch_1_fun/ppermute | solution.py:664
  21.7 15.7 %copy-start.44 = (s32[2,96]{1,0:T(2,128)S(1)}, s32[2,96]{1,0:T(2,128)}, u32[]{:S(2)}) copy-start(s32[2,96]{1,0:T(2,128)} %get-tuple-element.138) | copy-start | bytes 2308 | tf_op jit(solution)/shard_map/cond
  22.5 0.7 collective-permute-start.27
  23.1 30.6 %copy-start.50 = (bf16[128,128]{1,0:T(8,128)(2,1)}, bf16[128,128]{1,0:T(8,128)(2,1)S(1)}, u32[]{:S(2)}) copy-start(bf16[128,128]{1,0:T(8,128)(2,1)S(1)} %collective-permute-done.27.head_ref) | copy-start | bytes 98308 | tf_op jit(solution)/shard_map/cond
  26.8 1.1 copy-start
  27.9 40.0 %collective-permute-start.31 = (bf16[6144,128]{1,0:T(8,128)(2,1)}, bf16[6144,128]{1,0:T(8,128)(2,1)S(1)}, u32[]{:S(2)}, u32[]{:S(2)}) collective-permute-start(bf16[6144,128]{1,0:T(8,128)(2,1)} %get-tuple-element.143), channel_id=1, source_target_pairs={{1,3},{5,7},{9,11},{13,15},{17,19},{21,23},{25,27},{29,31}} | collective-permute-start | bytes 4718600 | tf_op jit(solution)/shard_map/cond/branch_1_fun/ppermute | solution.py:649
  28.6 33.5 %collective-permute-start.34 = (bf16[2,290,8,128]{3,2,1,0:T(8,128)(2,1)}, bf16[2,290,8,128]{3,2,1,0:T(8,128)(2,1)}, u32[]{:S(2)}, u32[]{:S(2)}) collective-permute-start(bf16[2,290,8,128]{3,2,1,0:T(8,128)(2,1)} %get-tuple-element.148), channel_id=1, source_target_pairs={{5,4},{6,5},{7,6},{13,12},{14,13},{15,14},{21,20},{22,21},{23,22},... | collective-permute-start | bytes 3563528 | tf_op jit(solution)/shard_map/cond/branch_1_fun/ppermute | solution.py:664
  30.3 1.3 copy-start.1
  36.1 8.7 %collective-permute-start.28 = (f32[2,96,96]{2,1,0:T(8,128)S(1)}, f32[2,96,96]{2,1,0:T(8,128)S(1)}, u32[]{:S(2)}, u32[]{:S(2)}) collective-permute-start(f32[2,96,96]{2,1,0:T(8,128)S(1)} %face.8), channel_id=1, source_target_pairs={{0,1},{3,2},{8,9},{11,10},{16,17},{19,18},{24,25},{27,26}} | collective-permute-start | bytes 221192 | tf_op jit(solution)/shard_map/cond/branch_1_fun/ppermute | solution.py:687
  44.8 8.9 %copy-start.25 = (f32[2,96,96]{2,1,0:T(8,128)}, f32[2,96,96]{2,1,0:T(8,128)S(1)}, u32[]{:S(2)}) copy-start(f32[2,96,96]{2,1,0:T(8,128)S(1)} %add.73.rest_0_.refs_2_) | copy-start | bytes 221188 | tf_op jit(solution)/shard_map/cond
  44.8 8.9 %collective-permute-start.29 = (f32[2,96,96]{2,1,0:T(8,128)S(1)}, f32[2,96,96]{2,1,0:T(8,128)S(1)}, u32[]{:S(2)}, u32[]{:S(2)}) collective-permute-start(f32[2,96,96]{2,1,0:T(8,128)S(1)} %add.73.rest_0_.refs_2_), channel_id=1, source_target_pairs={{2,1},{10,9},{18,17},{26,25}} | collective-permute-start | bytes 221192 | tf_op jit(solution)/shard_map/cond/branch_1_fun/ppermute | solution.py:687
  53.8 0.6 copy-start.28
  56.1 2.5 %collective-permute-start.32 = (f32[128,128]{1,0:T(8,128)}, f32[128,128]{1,0:T(8,128)S(1)}, u32[]{:S(2)}, u32[]{:S(2)}) collective-permute-start(f32[128,128]{1,0:T(8,128)} %assemble.4), channel_id=1, source_target_pairs={{0,16},{9,25},{18,2},{27,11}} | collective-permute-start | bytes 196616 | tf_op jit(solution)/shard_map/cond/branch_1_fun/ppermute | solution.py:743
  59.5 6.2 %collective-permute-start.33 = (f32[128,128]{1,0:T(8,128)S(1)}, f32[128,128]{1,0:T(8,128)S(1)}, u32[]{:S(2)}, u32[]{:S(2)}) collective-permute-start(f32[128,128]{1,0:T(8,128)S(1)} %add.74), channel_id=1, source_target_pairs={{0,8},{16,24},{9,1},{25,17},{18,26},{2,10},{27,19},{11,3}} | collective-permute-start | bytes 196616 | tf_op jit(solution)/shard_map/cond/branch_1_fun/ppermute | solution.py:743
  60.8 20.2 %collective-permute-start.30 = (bf16[3072,128]{1,0:T(8,128)(2,1)}, bf16[3072,128]{1,0:T(8,128)(2,1)}, u32[]{:S(2)}, u32[]{:S(2)}) collective-permute-start(bf16[3072,128]{1,0:T(8,128)(2,1)} %copy-done.14), channel_id=1, source_target_pairs={{1,2},{5,6},{9,10},{13,14},{17,18},{21,22},{25,26},{29,30}} | collective-permute-start | bytes 2359304 | tf_op jit(solution)/shard_map/cond/branch_1_fun/ppermute | solution.py:649
  62.7 4.3 %collective-permute-start.36 = (f32[2,96,96]{2,1,0:T(8,128)S(1)}, f32[2,96,96]{2,1,0:T(8,128)S(1)}, u32[]{:S(2)}, u32[]{:S(2)}) collective-permute-start(f32[2,96,96]{2,1,0:T(8,128)S(1)} %face.9), channel_id=1, source_target_pairs={{4,5},{7,6},{12,13},{15,14},{20,21},{23,22},{28,29},{31,30}} | collective-permute-start | bytes 221192 | tf_op jit(solution)/shard_map/cond/branch_1_fun/ppermute | solution.py:687
  65.6 17.9 %copy-start.38 = (f32[128,128]{1,0:T(8,128)}, f32[128,128]{1,0:T(8,128)S(1)}, u32[]{:S(2)}) copy-start(f32[128,128]{1,0:T(8,128)S(1)} %add.75.refs_0_) | copy-start | bytes 196612 | tf_op jit(solution)/shard_map/cond
  65.6 2.2 %collective-permute-start.35 = (f32[128,128]{1,0:T(8,128)S(1)}, f32[128,128]{1,0:T(8,128)S(1)}, u32[]{:S(2)}, u32[]{:S(2)}) collective-permute-start(f32[128,128]{1,0:T(8,128)S(1)} %add.75.refs_0_), channel_id=1, source_target_pairs={{0,4},{8,12},{16,20},{24,28},{9,13},{1,5},{25,29},{17,21},{18,22},... | collective-permute-start | bytes 196616 | tf_op jit(solution)/shard_map/cond/branch_1_fun/ppermute | solution.py:743
  67.8 15.7 %copy-start.47 = (f32[128,128]{1,0:T(8,128)}, f32[128,128]{1,0:T(8,128)S(1)}, u32[]{:S(2)}) copy-start(f32[128,128]{1,0:T(8,128)S(1)} %collective-permute-done.35.refs_1_) | copy-start | bytes 196612 | tf_op jit(solution)/shard_map/cond
  67.8 54.2 %collective-permute-start.48 = (bf16[6144,128]{1,0:T(8,128)(2,1)S(1)}, bf16[6144,128]{1,0:T(8,128)(2,1)}, u32[]{:S(2)}, u32[]{:S(2)}) collective-permute-start(bf16[6144,128]{1,0:T(8,128)(2,1)S(1)} %collective-permute-done.31.rest_1_), channel_id=1, source_target_pairs={{3,2},{7,6},{11,10},{15,14},{19,18},{23,22},{27,26},{31,30}} | collective-permute-start | bytes 4718600 | tf_op jit(solution)/shard_map/cond/branch_1_fun/ppermute | solution.py:649
  69.1 21.2 %collective-permute-start.41 = (bf16[2048,128]{1,0:T(8,128)(2,1)}, bf16[2048,128]{1,0:T(8,128)(2,1)S(1)}, u32[]{:S(2)}, u32[]{:S(2)}) collective-permute-start(bf16[2048,128]{1,0:T(8,128)(2,1)} %slice.17), channel_id=1, source_target_pairs={{1,2},{5,6},{9,10},{13,14},{17,18},{21,22},{25,26},{29,30}} | collective-permute-start | bytes 1572872 | tf_op jit(solution)/shard_map/cond/branch_1_fun/ppermute | solution.py:649
  81.0 32.8 %collective-permute-start.47 = (bf16[3072,128]{1,0:T(8,128)(2,1)}, bf16[3072,128]{1,0:T(8,128)(2,1)S(1)}, u32[]{:S(2)}, u32[]{:S(2)}) collective-permute-start(bf16[3072,128]{1,0:T(8,128)(2,1)} %collective-permute-done.30.rest_0_), channel_id=1, source_target_pairs={{2,3},{6,7},{10,11},{14,15},{18,19},{22,23},{26,27},{30,31}} | collective-permute-start | bytes 2359304 | tf_op jit(solution)/shard_map/cond/branch_1_fun/ppermute | solution.py:649
  82.3 1.3 copy-start.32
  82.3 1.2 collective-permute-start.37
  83.6 0.6 copy-start.42
  86.0 8.5 %collective-permute-start.40 = (bf16[384,128]{1,0:T(8,128)(2,1)}, bf16[384,128]{1,0:T(8,128)(2,1)S(1)}, u32[]{:S(2)}, u32[]{:S(2)}) collective-permute-start(bf16[384,128]{1,0:T(8,128)(2,1)} %get-tuple-element.164.rest_0_), channel_id=1, source_target_pairs={{1,2},{5,6},{9,10},{13,14},{17,18},{21,22},{25,26},{29,30}} | collective-permute-start | bytes 294920 | tf_op jit(solution)/shard_map/cond/branch_1_fun/ppermute | solution.py:754
  87.3 7.2 %collective-permute-start.39 = (bf16[384,128]{1,0:T(8,128)(2,1)}, bf16[384,128]{1,0:T(8,128)(2,1)S(1)}, u32[]{:S(2)}, u32[]{:S(2)}) collective-permute-start(bf16[384,128]{1,0:T(8,128)(2,1)} %get-tuple-element.164.rest_0_), channel_id=1, source_target_pairs={{1,3},{5,7},{9,11},{13,15},{17,19},{21,23},{25,27},{29,31}} | collective-permute-start | bytes 294920 | tf_op jit(solution)/shard_map/cond/branch_1_fun/ppermute | solution.py:754
  90.3 4.3 %collective-permute-start.38 = (bf16[384,128]{1,0:T(8,128)(2,1)}, bf16[384,128]{1,0:T(8,128)(2,1)S(1)}, u32[]{:S(2)}, u32[]{:S(2)}) collective-permute-start(bf16[384,128]{1,0:T(8,128)(2,1)} %get-tuple-element.164.rest_0_), channel_id=1, source_target_pairs={{1,0},{5,4},{9,8},{13,12},{17,16},{21,20},{25,24},{29,28}} | collective-permute-start | bytes 294920 | tf_op jit(solution)/shard_map/cond/branch_1_fun/ppermute | solution.py:754
  96.1 2.3 %collective-permute-start.45 = (f32[128,128]{1,0:T(8,128)}, f32[128,128]{1,0:T(8,128)S(1)}, u32[]{:S(2)}, u32[]{:S(2)}) collective-permute-start(f32[128,128]{1,0:T(8,128)} %added.4), channel_id=1, source_target_pairs={{17,18},{25,27}} | collective-permute-start | bytes 196616 | tf_op jit(solution)/shard_map/cond/branch_1_fun/ppermute | solution.py:713
  98.5 14.6 %collective-permute-start.46 = (bf16[1024,128]{1,0:T(8,128)(2,1)}, bf16[1024,128]{1,0:T(8,128)(2,1)S(1)}, u32[]{:S(2)}, u32[]{:S(2)}) collective-permute-start(bf16[1024,128]{1,0:T(8,128)(2,1)} %slice.18), channel_id=1, source_target_pairs={{1,2},{5,6},{9,10},{13,14},{17,18},{21,22},{25,26},{29,30}} | collective-permute-start | bytes 786440 | tf_op jit(solution)/shard_map/cond/branch_1_fun/ppermute | solution.py:649
  99.7 31.3 %collective-permute-start.49 = (bf16[2048,128]{1,0:T(8,128)(2,1)S(1)}, bf16[2048,128]{1,0:T(8,128)(2,1)}, u32[]{:S(2)}, u32[]{:S(2)}) collective-permute-start(bf16[2048,128]{1,0:T(8,128)(2,1)S(1)} %collective-permute-done.41.rest_0_), channel_id=1, source_target_pairs={{2,3},{6,7},{10,11},{14,15},{18,19},{22,23},{26,27},{30,31}} | collective-permute-start | bytes 1572872 | tf_op jit(solution)/shard_map/cond/branch_1_fun/ppermute | solution.py:649
  110.4 20.0 %collective-permute-start.44 = (f32[2,96,96]{2,1,0:T(8,128)}, f32[2,96,96]{2,1,0:T(8,128)S(1)}, u32[]{:S(2)}, u32[]{:S(2)}) collective-permute-start(f32[2,96,96]{2,1,0:T(8,128)} %get-tuple-element.171.sum_ref), channel_id=1, source_target_pairs={{1,2},{5,6},{9,10},{13,14},{17,18},{21,22},{25,26},{29,30}} | collective-permute-start | bytes 221192 | tf_op jit(solution)/shard_map/cond/branch_1_fun/ppermute | solution.py:759
  113.1 17.3 %collective-permute-start.43 = (f32[2,96,96]{2,1,0:T(8,128)}, f32[2,96,96]{2,1,0:T(8,128)S(1)}, u32[]{:S(2)}, u32[]{:S(2)}) collective-permute-start(f32[2,96,96]{2,1,0:T(8,128)} %get-tuple-element.171.sum_ref), channel_id=1, source_target_pairs={{1,3},{5,7},{9,11},{13,15},{17,19},{21,23},{25,27},{29,31}} | collective-permute-start | bytes 221192 | tf_op jit(solution)/shard_map/cond/branch_1_fun/ppermute | solution.py:759
  113.7 16.7 %collective-permute-start.42 = (f32[2,96,96]{2,1,0:T(8,128)}, f32[2,96,96]{2,1,0:T(8,128)S(1)}, u32[]{:S(2)}, u32[]{:S(2)}) collective-permute-start(f32[2,96,96]{2,1,0:T(8,128)} %get-tuple-element.171.sum_ref), channel_id=1, source_target_pairs={{1,0},{5,4},{9,8},{13,12},{17,16},{21,20},{25,24},{29,28}} | collective-permute-start | bytes 221192 | tf_op jit(solution)/shard_map/cond/branch_1_fun/ppermute | solution.py:759
  114.5 0.8 copy-start.7
  115.3 0.9 copy-start.10
  117.2 6.1 %copy-start.16 = (bf16[12288,128]{1,0:T(8,128)(2,1)S(1)}, bf16[12288,128]{1,0:T(8,128)(2,1)}, u32[]{:S(2)}) copy-start(bf16[12288,128]{1,0:T(8,128)(2,1)} %get-tuple-element.119.slab_ref) | copy-start | bytes 9437188 | tf_op jit(solution)/shard_map/cond
  122.0 9.0 %collective-permute-start.50 = (bf16[1024,128]{1,0:T(8,128)(2,1)S(1)}, bf16[1024,128]{1,0:T(8,128)(2,1)S(1)}, u32[]{:S(2)}, u32[]{:S(2)}) collective-permute-start(bf16[1024,128]{1,0:T(8,128)(2,1)S(1)} %collective-permute-done.46.rest_2_), channel_id=1, source_target_pairs={{2,3},{6,7},{10,11},{14,15},{18,19},{22,23},{26,27},{30,31}} | collective-permute-start | bytes 786440 | tf_op jit(solution)/shard_map/cond/branch_1_fun/ppermute | solution.py:649
  123.4 7.0 %copy-start.34 = (f32[2,96,96]{2,1,0:T(8,128)S(1)}, f32[2,96,96]{2,1,0:T(8,128)}, u32[]{:S(2)}) copy-start(f32[2,96,96]{2,1,0:T(8,128)} %get-tuple-element.171.sum_ref) | copy-start | bytes 221188 | tf_op jit(solution)/shard_map/cond
  134.7 1.7 %copy-start.19 = (bf16[12288,128]{1,0:T(8,128)(2,1)}, bf16[12288,128]{1,0:T(8,128)(2,1)S(1)}, u32[]{:S(2)}) copy-start(bf16[12288,128]{1,0:T(8,128)(2,1)S(1)} %get-tuple-element.279) | copy-start | bytes 9437188 | tf_op jit(solution)/shard_map/cond
where the time goes:
time: 138 us; the launch traced here: 136 us
  Pallas kernels  42.8 us (31%)
  starting transfers between devices  42.4 us (31%)
  waiting for transfers between devices  32.9 us (24%)
  local copies, waits for them, and re-layouts  13 us (9%)
  other arithmetic  3.54 us (3%)
    ppermute x8, starting transfers between devices, send(): return lax.ppermute(value, 'narrow', [(owner + source, owner + target)])  19.1 us
    pallas_call x3, Pallas kernels, panel(): pl.pallas_call(functools.partial(panel_kernel, pieces=range(pieces), span...  15.4 us
    ppermute x8, waiting for transfers between devices, send(): return lax.ppermute(value, 'narrow', [(owner + source, owner + target)])  14.2 us
    pallas_call x1, Pallas kernels, interior(): pl.pallas_call(interior_kernel, grid=(subs, comps), in_specs=[SMEM, SMEM,...  10.7 us
    ppermute x4, starting transfers between devices, summed(): lax.ppermute(total, axes, within(group, pairs))  9.35 us
    ppermute x4, waiting for transfers between devices, summed(): lax.ppermute(total, axes, within(group, pairs))  8.24 us
    cond x34, local copies, waits for them, and re-layouts  7.93 us
    pallas_call x1, Pallas kernels, halo_message(): pl.pallas_call(functools.partial(halo_kernel, spans=spans), in_specs=[SME...  5.53 us
  transfers between devices with their start and end apart: 25, of which 9 were waited for; matrix products, arithmetic and copies ran while one was open for 6% of the time, Pallas kernels for 25%

commit v1 on v0

--- a/solution.py
+++ b/solution.py
@@ -578,7 +578,7 @@
         grid=(begin,),
         in_specs=blocks,
         out_specs=[pl.BlockSpec((tile, size), lambda i: (i + offset, 0)), SMEM],
-        out_shape=[jax.ShapeDtypeStruct(slab.shape, BF16), jax.ShapeDtypeStruct((1,), jnp.int32)],
+        out_shape=[pltpu.HBM(slab.shape, BF16), jax.ShapeDtypeStruct((1,), jnp.int32)],
         input_output_aliases=aliases,
         scratch_shapes=[
             pltpu.VMEM((2, tile, size), BF16),

time: 138 us -> 137 us (level)
  local copies, waits for them, and re-layouts: 13 us -> 11.4 us
    cond x34 -> x32, local copies, waits for them, and re-layouts: 7.93 us -> 6.29 us
where the time goes in v1:
time: 137 us; the launch traced here: 136 us
  Pallas kernels  43.5 us (32%)
  starting transfers between devices  42.5 us (31%)
  waiting for transfers between devices  32.7 us (24%)
  local copies, waits for them, and re-layouts  11.4 us (8%)
  other arithmetic  3.64 us (3%)
  between operations  1.48 us (1%)
    ppermute x8, starting transfers between devices, send(): return lax.ppermute(value, 'narrow', [(owner + source, owner + target)])  19.2 us
    pallas_call x3, Pallas kernels, panel(): pl.pallas_call(functools.partial(panel_kernel, pieces=range(pieces), span...  16.1 us
    ppermute x8, waiting for transfers between devices, send(): return lax.ppermute(value, 'narrow', [(owner + source, owner + target)])  14 us
    pallas_call x1, Pallas kernels, interior(): pl.pallas_call(interior_kernel, grid=(subs, comps), in_specs=[SMEM, SMEM,...  10.7 us
    ppermute x4, starting transfers between devices, summed(): lax.ppermute(total, axes, within(group, pairs))  9.35 us
    ppermute x4, waiting for transfers between devices, summed(): lax.ppermute(total, axes, within(group, pairs))  8.27 us
    cond x32, local copies, waits for them, and re-layouts  6.29 us
    pallas_call x1, Pallas kernels, halo_message(): pl.pallas_call(functools.partial(halo_kernel, spans=spans), in_specs=[SME...  5.53 us
  transfers between devices with their start and end apart: 25, of which 9 were waited for; matrix products, arithmetic and copies ran while one was open for 6% of the time, Pallas kernels for 25%

profile of v1, /device:TPU:22, one launch (start us, length us, event | category | flops | bytes accessed | tf_op | source)
XLA Modules:
  0.0 136.1 jit_solution(5423989885621895575)
XLA Ops:
  1.3 134.7 %conditional.1 = (bf16[12288,128]{1,0:T(8,128)(2,1)}, f32[2,96,96]{2,1,0:T(8,128)}) conditional(s32[]{:T(128)} %bitcast.33, (bf16[2,16]{1,0:T(2,128)(2,1)}, s32[2,4,8,128]{3,2,1,0:T(8,128)}, bf16[2,96,3,4,8,128]{5,4,3,2,1,0:T(8,128)(2,1)}, bf16[12288,128]{1,0:T(8,128)(2,1)}, s32[2,96]{1,0:T(2,128)}) %tuple.112, ...), branch_computations={%region_0.1_spmd, %region_1.2_spmd, %region_2.3_spmd} | conditional | flops 125047 | bytes 83196688 | solution.py:813
  2.0 5.5 %halo_message.4 = (bf16[2,290,8,128]{3,2,1,0:T(8,128)(2,1)}, bf16[2,288,8,128]{3,2,1,0:T(8,128)(2,1)S(1)}, bf16[6144,128]{1,0:T(8,128)(2,1)}, bf16[3072,128]{1,0:T(8,128)(2,1)S(1)}) custom-call(f32[2,16]{1,0:T(2,128)S(1)} %convert_element_type.2.table_ref, s32[2,4,8,128]{3,2,1,0:T(8,128)} %get-tuple-element.117.ids_ref, s32[1]{0:T(128)} %bitcast.11.token_ref.flags_ref, ...), custom_call_target="tpu_custom_call" | custom-call | flops 1 | bytes 1 | tf_op jit(solution)/shard_map/cond/branch_1_fun/halo_message/pallas_call | solution.py:94
  7.5 0.9 copy-done.14
  8.4 2.5 %collective-permute-start.26 = (bf16[2,290,8,128]{3,2,1,0:T(8,128)(2,1)}, bf16[2,290,8,128]{3,2,1,0:T(8,128)(2,1)S(1)}, u32[]{:S(2)}, u32[]{:S(2)}) collective-permute-start(bf16[2,290,8,128]{3,2,1,0:T(8,128)(2,1)} %get-tuple-element.148), channel_id=1, source_target_pairs={{1,0},{2,1},{3,2},{9,8},{10,9},{11,10},{17,16},{18,17},{19,18},{25... | collective-permute-start | bytes 3563528 | tf_op jit(solution)/shard_map/cond/branch_1_fun/ppermute | solution.py:664
  11.0 10.7 %interior.4.inner_ref = f32[2,96,96]{2,1,0:T(8,128)S(1)} custom-call(s32[1]{0:T(128)} %bitcast.17.edge_ref, f32[2,16]{1,0:T(2,128)S(1)} %convert_element_type.2.table_ref, s32[2,4,8,128]{3,2,1,0:T(8,128)S(1)} %copy-done.19, bf16[2,96,3,4,8,128]{5,4,3,2,1,0:T(8,128)(2,1)} %get-tuple-element.118.basis_ref, s32[1]{0:T(128)} %bitcast.11.token_ref.flags_ref), custom_call_target="tpu_custom_call" | custom-call | flops 1 | bytes 1 | tf_op jit(solution)/shard_map/cond/branch_1_fun/interior/pallas_call | solution.py:190
  21.7 0.8 slice.16
  23.1 3.6 %collective-permute-done.26.halo_ref = bf16[2,290,8,128]{3,2,1,0:T(8,128)(2,1)S(1)} collective-permute-done((bf16[2,290,8,128]{3,2,1,0:T(8,128)(2,1)}, bf16[2,290,8,128]{3,2,1,0:T(8,128)(2,1)S(1)}, u32[]{:S(2)}, u32[]{:S(2)}) %collective-permute-start.26) | collective-permute-done | bytes 1187872 | tf_op jit(solution)/shard_map/cond/branch_1_fun/ppermute | solution.py:664
  26.8 1.1 copy-done
  27.9 0.7 collective-permute-start.31
  28.6 1.7 %collective-permute-start.34 = (bf16[2,290,8,128]{3,2,1,0:T(8,128)(2,1)}, bf16[2,290,8,128]{3,2,1,0:T(8,128)(2,1)}, u32[]{:S(2)}, u32[]{:S(2)}) collective-permute-start(bf16[2,290,8,128]{3,2,1,0:T(8,128)(2,1)} %get-tuple-element.148), channel_id=1, source_target_pairs={{5,4},{6,5},{7,6},{13,12},{14,13},{15,14},{21,20},{22,21},{23,22},... | collective-permute-start | bytes 3563528 | tf_op jit(solution)/shard_map/cond/branch_1_fun/ppermute | solution.py:664
  30.3 1.3 copy-done.1
  31.6 4.5 %face.8 = f32[2,96,96]{2,1,0:T(8,128)S(1)} custom-call(s32[1]{0:T(128)} %bitcast.16.flags_ref, f32[2,16]{1,0:T(2,128)S(1)} %convert_element_type.2.table_ref, s32[2,4,8,128]{3,2,1,0:T(8,128)S(1)} %copy-done.19, bf16[2,288,8,128]{3,2,1,0:T(8,128)(2,1)S(1)} %get-tuple-element.121.last_ref, bf16[2,290,8,128]{3,2,1,0:T(8,128)(2,1)S(1)} %copy-done.1, ...), custom_call_target="tpu_custom_call" | custom-call | flops 1 | bytes 1 | tf_op jit(solution)/shard_map/cond/branch_1_fun/face/pallas_call | solution.py:268
  36.1 1.3 collective-permute-start.28
  37.4 0.8 copy.18.column_ids_ref
  38.2 6.7 %collective-permute-done.28 = f32[2,96,96]{2,1,0:T(8,128)S(1)} collective-permute-done((f32[2,96,96]{2,1,0:T(8,128)S(1)}, f32[2,96,96]{2,1,0:T(8,128)S(1)}, u32[]{:S(2)}, u32[]{:S(2)}) %collective-permute-start.28) | collective-permute-done | bytes 73760 | tf_op jit(solution)/shard_map/cond/branch_1_fun/ppermute | solution.py:687
  44.9 6.7 %collective-permute-start.29 = (f32[2,96,96]{2,1,0:T(8,128)S(1)}, f32[2,96,96]{2,1,0:T(8,128)S(1)}, u32[]{:S(2)}, u32[]{:S(2)}) collective-permute-start(f32[2,96,96]{2,1,0:T(8,128)S(1)} %add.73.rest_0_.refs_2_), channel_id=1, source_target_pairs={{2,1},{10,9},{18,17},{26,25}} | collective-permute-start | bytes 221192 | tf_op jit(solution)/shard_map/cond/branch_1_fun/ppermute | solution.py:687
  52.2 1.6 %collective-permute-done.29.rest_1_.refs_3_ = f32[2,96,96]{2,1,0:T(8,128)S(1)} collective-permute-done((f32[2,96,96]{2,1,0:T(8,128)S(1)}, f32[2,96,96]{2,1,0:T(8,128)S(1)}, u32[]{:S(2)}, u32[]{:S(2)}) %collective-permute-start.29) | collective-permute-done | bytes 73760 | tf_op jit(solution)/shard_map/cond/branch_1_fun/ppermute | solution.py:687
  54.4 1.7 %assemble.4 = f32[128,128]{1,0:T(8,128)} custom-call(s32[2]{0:T(128)} %pad_add_fusion.6.flags_ref, s32[1]{0:T(128)} %bitcast.11.token_ref.flags_ref, s32[2,96,1]{2,1,0:T(8,128)} %copy.18.column_ids_ref, s32[2,1,96]{2,1,0:T(1,128)S(1)} %bitcast.38, bf16[12288,128]{1,0:T(8,128)(2,1)} %get-tuple-element.119.slab_ref, bf16[128,128]{1,0:T(8,128)(2,1)} %copy-done.47, ...), custom_call_target="tpu_custom_call" | custom-call | flops 1 | bytes 1 | tf_op jit(solution)/shard_map/cond/branch_1_fun/assemble/pallas_call | solution.py:325
  56.8 1.9 %slice.17 = bf16[2048,128]{1,0:T(8,128)(2,1)} slice(bf16[12288,128]{1,0:T(8,128)(2,1)} %get-tuple-element.119.slab_ref), slice={[9216:11264], [0:128]} | slice | bytes 1048576 | tf_op jit(solution)/shard_map/cond/branch_1_fun/slice | solution.py:646
  58.6 0.9 add.74
  59.5 1.3 collective-permute-start.33
  60.8 1.3 collective-permute-start.30
  62.7 0.7 collective-permute-start.36
  63.4 2.3 %collective-permute-done.33 = f32[128,128]{1,0:T(8,128)S(1)} collective-permute-done((f32[128,128]{1,0:T(8,128)S(1)}, f32[128,128]{1,0:T(8,128)S(1)}, u32[]{:S(2)}, u32[]{:S(2)}) %collective-permute-start.33) | collective-permute-done | bytes 65568 | tf_op jit(solution)/shard_map/cond/branch_1_fun/ppermute | solution.py:743
  65.7 1.3 collective-permute-start.35
  67.0 0.9 collective-permute-done.35.refs_1_
  67.8 1.3 collective-permute-start.48
  69.1 1.3 collective-permute-start.41
  70.4 10.5 %collective-permute-done.30.rest_0_ = bf16[3072,128]{1,0:T(8,128)(2,1)} collective-permute-done((bf16[3072,128]{1,0:T(8,128)(2,1)}, bf16[3072,128]{1,0:T(8,128)(2,1)}, u32[]{:S(2)}, u32[]{:S(2)}) %collective-permute-start.30) | collective-permute-done | bytes 786464 | tf_op jit(solution)/shard_map/cond/branch_1_fun/ppermute | solution.py:649
  81.0 1.3 collective-permute-start.47
  83.0 0.7 pad_add_fusion.5.flags_ref
  84.3 1.8 %factorize.4 = (bf16[384,128]{1,0:T(8,128)(2,1)}, f32[128,128]{1,0:T(8,128)}, f32[2,96,96]{2,1,0:T(8,128)}) custom-call(s32[2]{0:T(128)} %pad_add_fusion.5.flags_ref, s32[1]{0:T(128)} %bitcast.11.token_ref.flags_ref, f32[128,128]{1,0:T(8,128)} %copy-done.35, f32[128,128]{1,0:T(8,128)} %copy-done.44, f32[2,96,96]{2,1,0:T(8,128)} %copy-done.22, ...), custom_call_target="tpu_custom_call" | custom-call | flops 1 | bytes 1 | tf_op jit(solution)/shard_map/cond/branch_1_fun/factorize/pallas_call | solution.py:397
  86.2 1.3 collective-permute-start.40
  88.1 2.1 %collective-permute-done.41.rest_0_ = bf16[2048,128]{1,0:T(8,128)(2,1)S(1)} collective-permute-done((bf16[2048,128]{1,0:T(8,128)(2,1)}, bf16[2048,128]{1,0:T(8,128)(2,1)S(1)}, u32[]{:S(2)}, u32[]{:S(2)}) %collective-permute-start.41) | collective-permute-done | bytes 524320 | tf_op jit(solution)/shard_map/cond/branch_1_fun/ppermute | solution.py:649
  91.0 3.6 %collective-permute-done.40.rest_1_ = bf16[384,128]{1,0:T(8,128)(2,1)S(1)} collective-permute-done((bf16[384,128]{1,0:T(8,128)(2,1)}, bf16[384,128]{1,0:T(8,128)(2,1)S(1)}, u32[]{:S(2)}, u32[]{:S(2)}) %collective-permute-start.40) | collective-permute-done | bytes 98336 | tf_op jit(solution)/shard_map/cond/branch_1_fun/ppermute | solution.py:754
  94.6 1.6 %added.4 = f32[128,128]{1,0:T(8,128)} custom-call(s32[1]{0:T(128)} %bitcast.11.token_ref.flags_ref, s32[1]{0:T(128)} %bitcast.11.token_ref.flags_ref, s32[2,96,1]{2,1,0:T(8,128)} %copy.18.column_ids_ref, s32[2,1,96]{2,1,0:T(1,128)S(1)} %bitcast.39, f32[2,96,96]{2,1,0:T(8,128)} %get-tuple-element.171.sum_ref), custom_call_target="tpu_custom_call" | custom-call | flops 1 | bytes 1 | tf_op jit(solution)/shard_map/cond/branch_1_fun/added/pallas_call | solution.py:468
  96.8 1.7 %slice.18 = bf16[1024,128]{1,0:T(8,128)(2,1)} slice(bf16[12288,128]{1,0:T(8,128)(2,1)} %get-tuple-element.119.slab_ref), slice={[11264:12288], [0:128]} | slice | bytes 524288 | tf_op jit(solution)/shard_map/cond/branch_1_fun/slice | solution.py:646
  98.5 1.3 collective-permute-start.46
  99.8 10.6 %collective-permute-start.49 = (bf16[2048,128]{1,0:T(8,128)(2,1)S(1)}, bf16[2048,128]{1,0:T(8,128)(2,1)}, u32[]{:S(2)}, u32[]{:S(2)}) collective-permute-start(bf16[2048,128]{1,0:T(8,128)(2,1)S(1)} %collective-permute-done.41.rest_0_), channel_id=1, source_target_pairs={{2,3},{6,7},{10,11},{14,15},{18,19},{22,23},{26,27},{30,31}} | collective-permute-start | bytes 1572872 | tf_op jit(solution)/shard_map/cond/branch_1_fun/ppermute | solution.py:649
  110.5 1.3 collective-permute-start.44
  111.7 1.3 collective-permute-done.46.rest_2_
  114.5 0.8 copy-done.7
  115.3 0.9 copy-done.10
  116.2 1.0 prepare.4
  117.2 5.0 %panel.11 = (bf16[12288,128]{1,0:T(8,128)(2,1)}, s32[1]{0:T(128)}) custom-call(s32[4]{0:T(128)S(1)} %pad_add_fusion.4.flags_ref, s32[1]{0:T(128)} %bitcast.11.token_ref.flags_ref, bf16[128,128]{1,0:T(8,128)(2,1)S(1)} %get-tuple-element.180.lower_ref, bf16[512,256]{1,0:T(8,128)(2,1)S(1)} %get-tuple-element.181.weights_ref, ...), custom_call_target="tpu_custom_call" | custom-call | flops 1 | bytes 1 | tf_op jit(solution)/shard_map/cond/branch_1_fun/panel/pallas_call | solution.py:576
  122.3 1.3 collective-permute-start.50
  123.6 7.3 %panel.12 = (bf16[12288,128]{1,0:T(8,128)(2,1)}, s32[1]{0:T(128)}) custom-call(s32[4]{0:T(128)S(1)} %pad_add_fusion.4.flags_ref, s32[1]{0:T(128)} %get-tuple-element.185.token_ref, bf16[128,128]{1,0:T(8,128)(2,1)S(1)} %get-tuple-element.180.lower_ref, bf16[512,256]{1,0:T(8,128)(2,1)S(1)} %get-tuple-element.181.weights_ref, ...), custom_call_target="tpu_custom_call", output_to_operand_aliasing={{0}: (9, {})} | custom-call | flops 1 | bytes 1 | tf_op jit(solution)/shard_map/cond/branch_1_fun/panel/pallas_call | solution.py:576
  131.6 3.8 %panel.13 = (bf16[12288,128]{1,0:T(8,128)(2,1)}, s32[1]{0:T(128)}) custom-call(s32[4]{0:T(128)S(1)} %pad_add_fusion.4.flags_ref, s32[1]{0:T(128)} %get-tuple-element.192.token_ref, bf16[128,128]{1,0:T(8,128)(2,1)S(1)} %get-tuple-element.180.lower_ref, bf16[512,256]{1,0:T(8,128)(2,1)S(1)} %get-tuple-element.181.weights_ref, ...), custom_call_target="tpu_custom_call", output_to_operand_aliasing={{0}: (11, {})} | custom-call | flops 1 | bytes 1 | tf_op jit(solution)/shard_map/cond/branch_1_fun/panel/pallas_call | solution.py:576
  (60 shorter events, 9.3 us)
Async XLA Ops:
  2.0 9.0 %copy-start.19 = (s32[2,4,8,128]{3,2,1,0:T(8,128)S(1)}, s32[2,4,8,128]{3,2,1,0:T(8,128)}, u32[]{:S(2)}) copy-start(s32[2,4,8,128]{3,2,1,0:T(8,128)} %get-tuple-element.117.ids_ref) | copy-start | bytes 98308 | tf_op jit(solution)/shard_map/cond
  7.5 0.9 copy-start.14
  8.4 18.4 %collective-permute-start.26 = (bf16[2,290,8,128]{3,2,1,0:T(8,128)(2,1)}, bf16[2,290,8,128]{3,2,1,0:T(8,128)(2,1)S(1)}, u32[]{:S(2)}, u32[]{:S(2)}) collective-permute-start(bf16[2,290,8,128]{3,2,1,0:T(8,128)(2,1)} %get-tuple-element.148), channel_id=1, source_target_pairs={{1,0},{2,1},{3,2},{9,8},{10,9},{11,10},{17,16},{18,17},{19,18},{25... | collective-permute-start | bytes 3563528 | tf_op jit(solution)/shard_map/cond/branch_1_fun/ppermute | solution.py:664
  21.7 15.7 %copy-start.41 = (s32[2,96]{1,0:T(2,128)S(1)}, s32[2,96]{1,0:T(2,128)}, u32[]{:S(2)}) copy-start(s32[2,96]{1,0:T(2,128)} %get-tuple-element.138) | copy-start | bytes 2308 | tf_op jit(solution)/shard_map/cond
  22.5 0.7 collective-permute-start.27
  23.1 30.6 %copy-start.47 = (bf16[128,128]{1,0:T(8,128)(2,1)}, bf16[128,128]{1,0:T(8,128)(2,1)S(1)}, u32[]{:S(2)}) copy-start(bf16[128,128]{1,0:T(8,128)(2,1)S(1)} %collective-permute-done.27.head_ref) | copy-start | bytes 98308 | tf_op jit(solution)/shard_map/cond
  26.8 1.1 copy-start
  27.9 40.0 %collective-permute-start.31 = (bf16[6144,128]{1,0:T(8,128)(2,1)}, bf16[6144,128]{1,0:T(8,128)(2,1)S(1)}, u32[]{:S(2)}, u32[]{:S(2)}) collective-permute-start(bf16[6144,128]{1,0:T(8,128)(2,1)} %get-tuple-element.143), channel_id=1, source_target_pairs={{1,3},{5,7},{9,11},{13,15},{17,19},{21,23},{25,27},{29,31}} | collective-permute-start | bytes 4718600 | tf_op jit(solution)/shard_map/cond/branch_1_fun/ppermute | solution.py:649
  28.6 33.5 %collective-permute-start.34 = (bf16[2,290,8,128]{3,2,1,0:T(8,128)(2,1)}, bf16[2,290,8,128]{3,2,1,0:T(8,128)(2,1)}, u32[]{:S(2)}, u32[]{:S(2)}) collective-permute-start(bf16[2,290,8,128]{3,2,1,0:T(8,128)(2,1)} %get-tuple-element.148), channel_id=1, source_target_pairs={{5,4},{6,5},{7,6},{13,12},{14,13},{15,14},{21,20},{22,21},{23,22},... | collective-permute-start | bytes 3563528 | tf_op jit(solution)/shard_map/cond/branch_1_fun/ppermute | solution.py:664
  30.3 1.3 copy-start.1
  36.1 8.8 %collective-permute-start.28 = (f32[2,96,96]{2,1,0:T(8,128)S(1)}, f32[2,96,96]{2,1,0:T(8,128)S(1)}, u32[]{:S(2)}, u32[]{:S(2)}) collective-permute-start(f32[2,96,96]{2,1,0:T(8,128)S(1)} %face.8), channel_id=1, source_target_pairs={{0,1},{3,2},{8,9},{11,10},{16,17},{19,18},{24,25},{27,26}} | collective-permute-start | bytes 221192 | tf_op jit(solution)/shard_map/cond/branch_1_fun/ppermute | solution.py:687
  44.9 8.9 %copy-start.22 = (f32[2,96,96]{2,1,0:T(8,128)}, f32[2,96,96]{2,1,0:T(8,128)S(1)}, u32[]{:S(2)}) copy-start(f32[2,96,96]{2,1,0:T(8,128)S(1)} %add.73.rest_0_.refs_2_) | copy-start | bytes 221188 | tf_op jit(solution)/shard_map/cond
  44.9 8.9 %collective-permute-start.29 = (f32[2,96,96]{2,1,0:T(8,128)S(1)}, f32[2,96,96]{2,1,0:T(8,128)S(1)}, u32[]{:S(2)}, u32[]{:S(2)}) collective-permute-start(f32[2,96,96]{2,1,0:T(8,128)S(1)} %add.73.rest_0_.refs_2_), channel_id=1, source_target_pairs={{2,1},{10,9},{18,17},{26,25}} | collective-permute-start | bytes 221192 | tf_op jit(solution)/shard_map/cond/branch_1_fun/ppermute | solution.py:687
  53.8 0.7 copy-start.25
  56.1 2.5 %collective-permute-start.32 = (f32[128,128]{1,0:T(8,128)}, f32[128,128]{1,0:T(8,128)S(1)}, u32[]{:S(2)}, u32[]{:S(2)}) collective-permute-start(f32[128,128]{1,0:T(8,128)} %assemble.4), channel_id=1, source_target_pairs={{0,16},{9,25},{18,2},{27,11}} | collective-permute-start | bytes 196616 | tf_op jit(solution)/shard_map/cond/branch_1_fun/ppermute | solution.py:743
  59.5 6.2 %collective-permute-start.33 = (f32[128,128]{1,0:T(8,128)S(1)}, f32[128,128]{1,0:T(8,128)S(1)}, u32[]{:S(2)}, u32[]{:S(2)}) collective-permute-start(f32[128,128]{1,0:T(8,128)S(1)} %add.74), channel_id=1, source_target_pairs={{0,8},{16,24},{9,1},{25,17},{18,26},{2,10},{27,19},{11,3}} | collective-permute-start | bytes 196616 | tf_op jit(solution)/shard_map/cond/branch_1_fun/ppermute | solution.py:743
  60.8 20.2 %collective-permute-start.30 = (bf16[3072,128]{1,0:T(8,128)(2,1)}, bf16[3072,128]{1,0:T(8,128)(2,1)}, u32[]{:S(2)}, u32[]{:S(2)}) collective-permute-start(bf16[3072,128]{1,0:T(8,128)(2,1)} %copy-done.14), channel_id=1, source_target_pairs={{1,2},{5,6},{9,10},{13,14},{17,18},{21,22},{25,26},{29,30}} | collective-permute-start | bytes 2359304 | tf_op jit(solution)/shard_map/cond/branch_1_fun/ppermute | solution.py:649
  62.7 4.3 %collective-permute-start.36 = (f32[2,96,96]{2,1,0:T(8,128)S(1)}, f32[2,96,96]{2,1,0:T(8,128)S(1)}, u32[]{:S(2)}, u32[]{:S(2)}) collective-permute-start(f32[2,96,96]{2,1,0:T(8,128)S(1)} %face.9), channel_id=1, source_target_pairs={{4,5},{7,6},{12,13},{15,14},{20,21},{23,22},{28,29},{31,30}} | collective-permute-start | bytes 221192 | tf_op jit(solution)/shard_map/cond/branch_1_fun/ppermute | solution.py:687
  65.7 18.0 %copy-start.35 = (f32[128,128]{1,0:T(8,128)}, f32[128,128]{1,0:T(8,128)S(1)}, u32[]{:S(2)}) copy-start(f32[128,128]{1,0:T(8,128)S(1)} %add.75.refs_0_) | copy-start | bytes 196612 | tf_op jit(solution)/shard_map/cond
  65.7 2.2 %collective-permute-start.35 = (f32[128,128]{1,0:T(8,128)S(1)}, f32[128,128]{1,0:T(8,128)S(1)}, u32[]{:S(2)}, u32[]{:S(2)}) collective-permute-start(f32[128,128]{1,0:T(8,128)S(1)} %add.75.refs_0_), channel_id=1, source_target_pairs={{0,4},{8,12},{16,20},{24,28},{9,13},{1,5},{25,29},{17,21},{18,22},... | collective-permute-start | bytes 196616 | tf_op jit(solution)/shard_map/cond/branch_1_fun/ppermute | solution.py:743
  67.8 15.9 %copy-start.44 = (f32[128,128]{1,0:T(8,128)}, f32[128,128]{1,0:T(8,128)S(1)}, u32[]{:S(2)}) copy-start(f32[128,128]{1,0:T(8,128)S(1)} %collective-permute-done.35.refs_1_) | copy-start | bytes 196612 | tf_op jit(solution)/shard_map/cond
  67.8 54.4 %collective-permute-start.48 = (bf16[6144,128]{1,0:T(8,128)(2,1)S(1)}, bf16[6144,128]{1,0:T(8,128)(2,1)}, u32[]{:S(2)}, u32[]{:S(2)}) collective-permute-start(bf16[6144,128]{1,0:T(8,128)(2,1)S(1)} %collective-permute-done.31.rest_1_), channel_id=1, source_target_pairs={{3,2},{7,6},{11,10},{15,14},{19,18},{23,22},{27,26},{31,30}} | collective-permute-start | bytes 4718600 | tf_op jit(solution)/shard_map/cond/branch_1_fun/ppermute | solution.py:649
  69.1 21.2 %collective-permute-start.41 = (bf16[2048,128]{1,0:T(8,128)(2,1)}, bf16[2048,128]{1,0:T(8,128)(2,1)S(1)}, u32[]{:S(2)}, u32[]{:S(2)}) collective-permute-start(bf16[2048,128]{1,0:T(8,128)(2,1)} %slice.17), channel_id=1, source_target_pairs={{1,2},{5,6},{9,10},{13,14},{17,18},{21,22},{25,26},{29,30}} | collective-permute-start | bytes 1572872 | tf_op jit(solution)/shard_map/cond/branch_1_fun/ppermute | solution.py:649
  81.0 32.7 %collective-permute-start.47 = (bf16[3072,128]{1,0:T(8,128)(2,1)}, bf16[3072,128]{1,0:T(8,128)(2,1)S(1)}, u32[]{:S(2)}, u32[]{:S(2)}) collective-permute-start(bf16[3072,128]{1,0:T(8,128)(2,1)} %collective-permute-done.30.rest_0_), channel_id=1, source_target_pairs={{2,3},{6,7},{10,11},{14,15},{18,19},{22,23},{26,27},{30,31}} | collective-permute-start | bytes 2359304 | tf_op jit(solution)/shard_map/cond/branch_1_fun/ppermute | solution.py:649
  82.3 1.4 %copy-start.29 = (f32[2,96,96]{2,1,0:T(8,128)}, f32[2,96,96]{2,1,0:T(8,128)S(1)}, u32[]{:S(2)}) copy-start(f32[2,96,96]{2,1,0:T(8,128)S(1)} %add.76.refs_4_) | copy-start | bytes 221188 | tf_op jit(solution)/shard_map/cond
  82.3 1.3 collective-permute-start.37
  83.7 0.6 copy-start.39
  86.2 8.4 %collective-permute-start.40 = (bf16[384,128]{1,0:T(8,128)(2,1)}, bf16[384,128]{1,0:T(8,128)(2,1)S(1)}, u32[]{:S(2)}, u32[]{:S(2)}) collective-permute-start(bf16[384,128]{1,0:T(8,128)(2,1)} %get-tuple-element.164.rest_0_), channel_id=1, source_target_pairs={{1,2},{5,6},{9,10},{13,14},{17,18},{21,22},{25,26},{29,30}} | collective-permute-start | bytes 294920 | tf_op jit(solution)/shard_map/cond/branch_1_fun/ppermute | solution.py:754
  87.5 7.1 %collective-permute-start.39 = (bf16[384,128]{1,0:T(8,128)(2,1)}, bf16[384,128]{1,0:T(8,128)(2,1)S(1)}, u32[]{:S(2)}, u32[]{:S(2)}) collective-permute-start(bf16[384,128]{1,0:T(8,128)(2,1)} %get-tuple-element.164.rest_0_), channel_id=1, source_target_pairs={{1,3},{5,7},{9,11},{13,15},{17,19},{21,23},{25,27},{29,31}} | collective-permute-start | bytes 294920 | tf_op jit(solution)/shard_map/cond/branch_1_fun/ppermute | solution.py:754
  90.3 4.3 %collective-permute-start.38 = (bf16[384,128]{1,0:T(8,128)(2,1)}, bf16[384,128]{1,0:T(8,128)(2,1)S(1)}, u32[]{:S(2)}, u32[]{:S(2)}) collective-permute-start(bf16[384,128]{1,0:T(8,128)(2,1)} %get-tuple-element.164.rest_0_), channel_id=1, source_target_pairs={{1,0},{5,4},{9,8},{13,12},{17,16},{21,20},{25,24},{29,28}} | collective-permute-start | bytes 294920 | tf_op jit(solution)/shard_map/cond/branch_1_fun/ppermute | solution.py:754
  96.1 2.3 %collective-permute-start.45 = (f32[128,128]{1,0:T(8,128)}, f32[128,128]{1,0:T(8,128)S(1)}, u32[]{:S(2)}, u32[]{:S(2)}) collective-permute-start(f32[128,128]{1,0:T(8,128)} %added.4), channel_id=1, source_target_pairs={{17,18},{25,27}} | collective-permute-start | bytes 196616 | tf_op jit(solution)/shard_map/cond/branch_1_fun/ppermute | solution.py:713
  98.5 14.6 %collective-permute-start.46 = (bf16[1024,128]{1,0:T(8,128)(2,1)}, bf16[1024,128]{1,0:T(8,128)(2,1)S(1)}, u32[]{:S(2)}, u32[]{:S(2)}) collective-permute-start(bf16[1024,128]{1,0:T(8,128)(2,1)} %slice.18), channel_id=1, source_target_pairs={{1,2},{5,6},{9,10},{13,14},{17,18},{21,22},{25,26},{29,30}} | collective-permute-start | bytes 786440 | tf_op jit(solution)/shard_map/cond/branch_1_fun/ppermute | solution.py:649
  99.8 31.9 %collective-permute-start.49 = (bf16[2048,128]{1,0:T(8,128)(2,1)S(1)}, bf16[2048,128]{1,0:T(8,128)(2,1)}, u32[]{:S(2)}, u32[]{:S(2)}) collective-permute-start(bf16[2048,128]{1,0:T(8,128)(2,1)S(1)} %collective-permute-done.41.rest_0_), channel_id=1, source_target_pairs={{2,3},{6,7},{10,11},{14,15},{18,19},{22,23},{26,27},{30,31}} | collective-permute-start | bytes 1572872 | tf_op jit(solution)/shard_map/cond/branch_1_fun/ppermute | solution.py:649
  110.5 20.5 %collective-permute-start.44 = (f32[2,96,96]{2,1,0:T(8,128)}, f32[2,96,96]{2,1,0:T(8,128)S(1)}, u32[]{:S(2)}, u32[]{:S(2)}) collective-permute-start(f32[2,96,96]{2,1,0:T(8,128)} %get-tuple-element.171.sum_ref), channel_id=1, source_target_pairs={{1,2},{5,6},{9,10},{13,14},{17,18},{21,22},{25,26},{29,30}} | collective-permute-start | bytes 221192 | tf_op jit(solution)/shard_map/cond/branch_1_fun/ppermute | solution.py:759
  113.0 17.9 %collective-permute-start.43 = (f32[2,96,96]{2,1,0:T(8,128)}, f32[2,96,96]{2,1,0:T(8,128)S(1)}, u32[]{:S(2)}, u32[]{:S(2)}) collective-permute-start(f32[2,96,96]{2,1,0:T(8,128)} %get-tuple-element.171.sum_ref), channel_id=1, source_target_pairs={{1,3},{5,7},{9,11},{13,15},{17,19},{21,23},{25,27},{29,31}} | collective-permute-start | bytes 221192 | tf_op jit(solution)/shard_map/cond/branch_1_fun/ppermute | solution.py:759
  113.7 17.3 %collective-permute-start.42 = (f32[2,96,96]{2,1,0:T(8,128)}, f32[2,96,96]{2,1,0:T(8,128)S(1)}, u32[]{:S(2)}, u32[]{:S(2)}) collective-permute-start(f32[2,96,96]{2,1,0:T(8,128)} %get-tuple-element.171.sum_ref), channel_id=1, source_target_pairs={{1,0},{5,4},{9,8},{13,12},{17,16},{21,20},{25,24},{29,28}} | collective-permute-start | bytes 221192 | tf_op jit(solution)/shard_map/cond/branch_1_fun/ppermute | solution.py:759
  114.5 0.8 copy-start.7
  115.3 0.9 copy-start.10
  117.2 6.4 %copy-start.16 = (bf16[12288,128]{1,0:T(8,128)(2,1)S(1)}, bf16[12288,128]{1,0:T(8,128)(2,1)}, u32[]{:S(2)}) copy-start(bf16[12288,128]{1,0:T(8,128)(2,1)} %get-tuple-element.119.slab_ref) | copy-start | bytes 9437188 | tf_op jit(solution)/shard_map/cond
  122.3 9.4 %collective-permute-start.50 = (bf16[1024,128]{1,0:T(8,128)(2,1)S(1)}, bf16[1024,128]{1,0:T(8,128)(2,1)S(1)}, u32[]{:S(2)}, u32[]{:S(2)}) collective-permute-start(bf16[1024,128]{1,0:T(8,128)(2,1)S(1)} %collective-permute-done.46.rest_2_), channel_id=1, source_target_pairs={{2,3},{6,7},{10,11},{14,15},{18,19},{22,23},{26,27},{30,31}} | collective-permute-start | bytes 786440 | tf_op jit(solution)/shard_map/cond/branch_1_fun/ppermute | solution.py:649
  123.6 7.4 %copy-start.31 = (f32[2,96,96]{2,1,0:T(8,128)S(1)}, f32[2,96,96]{2,1,0:T(8,128)}, u32[]{:S(2)}) copy-start(f32[2,96,96]{2,1,0:T(8,128)} %get-tuple-element.171.sum_ref) | copy-start | bytes 221188 | tf_op jit(solution)/shard_map/cond
